TPU v7x, 256 devices: a whole 4x4x8 slice. The times are simulated.
256 devices in a mesh: front: 2 (over y_lo), row: 8 (over y_hi, x), col: 16 (over z, core).
Axes of the slice: x: 4, y: 4 (y_hi: 2, y_lo: 2; y = y_hi * 2 + y_lo), z: 8, core: 2. Of those that a mesh axis runs over, the one named last changes fastest.
Arguments:
- front_orig: bfloat16 [2, 12288, 12288], P('front', 'row', 'col'), as said below
- child_update: bfloat16 [8192, 32768], P(('front', 'row'), 'col'), as said below
- tile_map: int32 [2, 2, 64], replicated, may hold values from 0 to 95, as said below
Outputs:
- update: float32 [2, 12288, 12288], P('front', 'row', 'col')
- factor: float32 [2, 12288, 512], P('front', 'row')
Inputs may be any that keep to these rules, and one draw needn't show every extreme that they name: For every f and c, tile_map[f, c] is one-to-one. tile_map[f, c, i] mod 16 depends only on i mod 16 and takes each of its 16 values once over 16 consecutive i; tile_map[f, c, i] mod 8 depends only on i mod 8. `front_orig`: each front is symmetric in logical order. `child_update`: each child's 8192 x 8192 matrix is symmetric.
All inputs are finite; a program needn't handle non-finite values.
Results may differ from a plain program's by a relative error of at most 0.0009.
Values may be sent and summed in bfloat16 or wider, within the bound.
No kernel may reach another device: no remote copies, remote signals or barrier semaphores. Data moves between devices by JAX's collectives and lax.ppermute only.
A program may use at most 128 MiB of HBM per device.

v0:
```python
import jax
import jax.numpy as jnp
from jax import lax
from jax.sharding import PartitionSpec as P

TILE = 128
PANELS = 2
PANEL = 256
NT = 96
NCT = 64


def from_partner(block, axis, apart):
    count = lax.axis_size(axis)
    route = []
    for low in range(count):
        high = low | 1 << apart
        if high != low and high < count:
            route += [(low, high), (high, low)]
    return lax.ppermute(block, axis, route)


def broadcast(block, axis, holder):
    block = jnp.where(lax.axis_index(axis) == holder, block, jnp.zeros_like(block))
    return lax.psum(block, axis)


def dot_high(left_mat, right_mat):
    return lax.dot_general(
        left_mat,
        right_mat,
        (((1,), (1,)), ((), ())),
        precision=lax.Precision.HIGHEST,
        preferred_element_type=jnp.float32,
    )


def per_device(front_orig, child_update, tile_map):
    row_count = lax.axis_size("row")
    col_count = lax.axis_size("col")
    front_id = lax.axis_index("front")
    row_id = lax.axis_index("row")
    col_id = lax.axis_index("col")
    local_rt = NT // row_count
    local_ct = NT // col_count
    band_rows = NCT // (2 * row_count)
    band_cols = 4 * NCT // col_count
    cap_rows = max(1, band_rows // row_count)
    cap_cols = max(1, band_cols // col_count)
    capacity = cap_rows * cap_cols
    half_cols = col_count // 2
    quarter = col_count // 4
    peer_count = row_count * col_count
    tile_stack = (
        child_update.reshape(band_rows, TILE, band_cols, TILE)
        .transpose(0, 2, 1, 3)
        .reshape(band_rows * band_cols, TILE, TILE)
    )
    along_rows = jnp.arange(band_rows)[:, None]
    along_cols = jnp.arange(band_cols)[None, :]
    child_no = col_id // quarter
    sender_map = tile_map[child_no // 2, child_no % 2]
    mapped_rows = sender_map[(front_id * row_count + row_id) * band_rows + along_rows]
    mapped_cols = sender_map[col_id % quarter * band_cols + along_cols]
    destination = mapped_rows % row_count * col_count + mapped_cols % col_count
    slot_no = along_rows // row_count * cap_cols + along_cols // col_count
    placement = (destination * capacity + slot_no).reshape(-1)
    outgoing = (
        jnp.zeros((peer_count * capacity, TILE, TILE), jnp.bfloat16).at[placement].set(tile_stack)
    )
    arrived = lax.all_to_all(outgoing, ("row", "col"), split_axis=0, concat_axis=0, tiled=True)
    arrived = arrived.reshape(row_count, 2, half_cols, capacity, TILE, TILE)
    kept = lax.dynamic_index_in_dim(arrived, front_id, 1, keepdims=False)
    leaving = lax.dynamic_index_in_dim(arrived, 1 - front_id, 1, keepdims=False)
    incoming = from_partner(leaving, "front", 0)
    slot_count = 2 * row_count * half_cols * capacity
    received = jnp.stack([kept, incoming]).reshape(slot_count, TILE, TILE)
    own_maps = lax.dynamic_index_in_dim(tile_map, front_id, 0, keepdims=False)
    source_side = jnp.arange(2)[:, None, None, None, None]
    source_row = jnp.arange(row_count)[None, :, None, None, None]
    source_col = jnp.arange(half_cols)[None, None, :, None, None]
    tile_row = jnp.arange(band_rows)[None, None, None, :, None]
    tile_col = jnp.arange(band_cols)[None, None, None, None, :]
    source_front = jnp.where(source_side == 0, front_id, 1 - front_id)
    sibling = source_col // quarter
    got_rows = own_maps[sibling, (source_front * row_count + source_row) * band_rows + tile_row]
    got_cols = own_maps[sibling, source_col % quarter * band_cols + tile_col]
    is_mine = (got_rows % row_count == row_id) & (got_cols % col_count == col_id)
    position = (
        ((source_side * row_count + source_row) * half_cols + source_col) * capacity
        + tile_row // row_count * cap_cols
        + tile_col // col_count
    )
    target = got_rows // row_count * local_ct + got_cols // col_count
    spare_tile = local_rt * local_ct
    position = jnp.where(is_mine, position, slot_count)
    slot_table = (
        jnp.full((slot_count,), spare_tile, jnp.int32)
        .at[position.reshape(-1)]
        .set(target.reshape(-1), mode="drop")
    )
    tile_sums = (
        front_orig[0]
        .astype(jnp.float32)
        .reshape(local_rt, TILE, local_ct, TILE)
        .transpose(0, 2, 1, 3)
        .reshape(spare_tile, TILE, TILE)
    )
    tile_sums = jnp.concatenate([tile_sums, jnp.zeros((1, TILE, TILE), jnp.float32)])
    tile_sums = tile_sums.at[slot_table].add(received.astype(jnp.float32))
    front_mat = (
        tile_sums[:spare_tile]
        .reshape(local_rt, local_ct, TILE, TILE)
        .transpose(0, 2, 1, 3)
        .reshape(local_rt * TILE, local_ct * TILE)
    )
    row_tiles = jnp.repeat(row_id + row_count * jnp.arange(local_rt), TILE)
    ratio = col_count // row_count
    offset = (col_id - row_id) // row_count % ratio
    identity = jnp.eye(PANEL, dtype=jnp.float32)
    columns = []
    for panel_no in range(PANELS):
        halves = []
        for side_no in range(2):
            halves.append(broadcast(front_mat[:, :TILE], "col", 2 * panel_no + side_no))
        strip_cols = jnp.concatenate(halves, axis=1)
        block_rows = []
        for side_no in range(2):
            tile_no = 2 * panel_no + side_no
            local_no = tile_no // row_count
            rows_here = strip_cols[local_no * TILE : (local_no + 1) * TILE]
            block_rows.append(jnp.where(row_id == tile_no % row_count, rows_here, 0.0))
        diagonal = lax.psum(jnp.concatenate(block_rows, axis=0), "row")
        lower_f = jnp.linalg.cholesky(diagonal)
        inverse = jax.scipy.linalg.solve_triangular(lower_f, identity, lower=True)
        panel_cols = dot_high(strip_cols, inverse)
        panel_cols = jnp.where((row_tiles >= 2 * panel_no)[:, None], panel_cols, 0.0)
        columns.append(panel_cols)
        trail_rows = jnp.where((row_tiles >= 2 * panel_no + 2)[:, None], panel_cols, 0.0)
        picked = lax.dynamic_index_in_dim(
            trail_rows.reshape(local_ct, ratio, TILE, PANEL), offset, 1, keepdims=False
        )
        picked = picked.reshape(local_ct * TILE, PANEL)
        trail_cols = broadcast(picked.astype(jnp.bfloat16), "row", col_id % row_count).astype(
            picked.dtype
        )
        front_mat = front_mat - dot_high(trail_rows, trail_cols)
    return (front_mat[None], jnp.concatenate(columns, axis=1)[None])


def solution(mesh):
    placed = (P("front", "row", "col"), P(("front", "row"), "col"), P())
    return jax.shard_map(
        per_device,
        mesh=mesh,
        in_specs=placed,
        out_specs=(P("front", "row", "col"), P("front", "row", None)),
        check_vma=False,
    )
```

profile of v0, /device:TPU:32, one launch (start us, length us, event | category | flops | bytes accessed | tf_op | source)
XLA Modules:
  0.0 993.6 jit_solution(12782140775272528399)
XLA Ops:
  9.4 2.2 copy.33
  12.5 3.1 broadcast_in_dim.113
  15.6 8.6 scatter_fusion
  24.2 15.5 %all-to-all-start = ((bf16[128,128,128]{2,1,0:T(8,128)(2,1)}), bf16[128,128,128]{2,1,0:T(8,128)(2,1)}, u32[]{:S(2)}, u32[]{:S(2)}) async-start(bf16[128,128,128]{2,1,0:T(8,128)(2,1)} %scatter_fusion), calls=%async_computation | async-start | bytes 8388608 | tf_op jit(solution)/shard_map/all_to_all | solution.py:71
  40.1 4.8 gather_fusion
  45.2 1.5 gather_fusion.1
  48.2 4.8 convert_element_type.26
  53.0 2.1 copy.19
  55.1 82.4 %all-to-all-done = bf16[128,128,128]{2,1,0:T(8,128)(2,1)} async-done(((bf16[128,128,128]{2,1,0:T(8,128)(2,1)}), bf16[128,128,128]{2,1,0:T(8,128)(2,1)}, u32[]{:S(2)}, u32[]{:S(2)}) %all-to-all-start) | async-done | bytes 4194336 | tf_op jit(solution)/shard_map/all_to_all | solution.py:71
  137.5 5.0 dynamic-slice_bitcast_fusion.1
  142.5 0.7 collective-permute-start
  143.2 30.7 %scatter_custom_fusion = s32[128]{0:T(128)S(1)} fusion(s32[8192]{0:T(1024)S(1)} %bitcast.145, s32[8192]{0:T(1024)S(1)} %reshape.847, s32[]{:T(128)} %constant.303.clone.1), kind=kCustom, calls=%fused_computation.185 | custom fusion | bytes 516 | tf_op jit(solution)/shard_map/scatter | solution.py:100
  173.9 2.8 pad_convert_fusion
  176.8 13.2 %collective-permute-done = bf16[8,8,1,128,128]{4,3,1,0,2:T(8,128)(2,1)} collective-permute-done((bf16[8,8,1,128,128]{4,3,1,0,2:T(8,128)(2,1)}, bf16[8,8,1,128,128]{4,3,1,0,2:T(8,128)(2,1)}, u32[]{:S(2)}, u32[]{:S(2)}) %collective-permute-start) | collective-permute-done | bytes 2097184 | tf_op jit(solution)/shard_map/ppermute | solution.py:20
  189.9 2.0 pad_maximum_fusion
  191.9 4.6 bitcast_convert_fusion
  196.5 25.5 %scatter_fusion.1 = f32[73,128,128]{2,1,0:T(8,128)} fusion(f32[73,128,128]{2,1,0:T(8,128)} %pad_convert_fusion, s32[128]{0:T(128)S(1)} %compare_select_fusion.6, f32[128,128,128]{2,1,0:T(8,128)} %bitcast_convert_fusion), kind=kCustom, calls=%fused_computation.6 | custom fusion | flops 2097152 | bytes 25166336 | tf_op jit(solution)/shard_map/scatter-add | solution.py:110
  222.0 5.1 slice.82
  227.1 6.6 copy.31
  233.7 5.1 copy.36
  238.8 2.2 copy-done.2
  240.9 1.4 slice_select_fusion.2
  242.5 106.6 %all-reduce.21.cloned.1.call-done = (f32[1536,128]{0,1:T(8,128)}, f32[1536,128]{0,1:T(8,128)}) async-done(((f32[1536,128]{0,1:T(8,128)}, f32[1536,128]{0,1:T(8,128)}), (f32[1536,128]{0,1:T(8,128)}, f32[1536,128]{0,1:T(8,128)})) %all-reduce.21.cloned.1.call-update) | async-done | bytes 1572880 | tf_op jit(solution)/shard_map/psum | solution.py:25
  349.1 1.3 constant_dynamic-update-slice_fusion.1
  350.5 1.1 copy-done.6
  351.7 0.7 pad_maximum_fusion.1
  353.1 92.0 %all-reduce.11.cloned.1.call-done = f32[256,256]{0,1:T(8,128)} async-done(((f32[256,256]{0,1:T(8,128)}), f32[256,256]{0,1:T(8,128)}) %all-reduce.11.cloned.1.call-update) | async-done | bytes 262160 | tf_op jit(solution)/shard_map/psum | solution.py:133
  445.2 1.1 copy.23
  446.2 1.0 fusion.9
  447.2 11.7 %cholesky.130 = f32[128,128]{1,0:T(8,128)S(1)} custom-call(f32[128,128]{1,0:T(8,128)S(1)} %cholesky.194), custom_call_target="Cholesky" | custom-call | tf_op jit(solution)/shard_map/jit(cholesky)/cholesky | solution.py:134
  459.0 9.8 custom-call.17
  469.3 11.7 %cholesky.147 = f32[128,128]{1,0:T(8,128)S(1)} custom-call(f32[128,128]{1,0:T(8,128)S(1)} %convolution_subtract_fusion.4), custom_call_target="Cholesky" | custom-call | tf_op jit(solution)/shard_map/jit(cholesky)/cholesky | solution.py:134
  481.1 0.7 compare_reduce_fusion.2
  483.8 4.1 while.4
  484.6 1.3 bitcast_dynamic-update-slice_fusion.4
  486.5 1.3 bitcast_dynamic-update-slice_fusion.4
  487.8 19.7 %custom-call.18 = f32[2,128,128]{1,2,0:T(8,128)S(1)} custom-call(f32[2,128,128]{2,1,0:T(8,128)S(1)} %get-tuple-element.18), custom_call_target="InvertDiagBlocksLowerTriangular" | custom-call | tf_op jit(solution)/shard_map/jit(_solve_triangular)/triangular_solve | solution.py:135
  508.4 4.6 broadcast_select_fusion.1
  513.1 0.8 fusion
  513.9 88.3 %all-reduce.13.cloned.1.call-done = bf16[768,256]{1,0:T(8,128)(2,1)} async-done(((bf16[768,256]{1,0:T(8,128)(2,1)}), bf16[768,256]{1,0:T(8,128)(2,1)}) %all-reduce.13.cloned.1.call-update) | async-done | bytes 393232 | tf_op jit(solution)/shard_map/psum | solution.py:25
  602.2 4.8 convolution_subtract_fusion
  607.1 2.2 copy-done.3
  609.2 1.3 slice_select_fusion
  610.6 108.9 %all-reduce.19.cloned.1.call-done = (f32[1536,128]{0,1:T(8,128)}, f32[1536,128]{0,1:T(8,128)}) async-done(((f32[1536,128]{0,1:T(8,128)}, f32[1536,128]{0,1:T(8,128)}), (f32[1536,128]{0,1:T(8,128)}, f32[1536,128]{0,1:T(8,128)})) %all-reduce.19.cloned.1.call-update) | async-done | bytes 1572880 | tf_op jit(solution)/shard_map/psum | solution.py:25
  719.5 1.3 constant_dynamic-update-slice_fusion.3
  721.0 1.1 copy-done.7
  722.1 0.7 pad_maximum_fusion.2
  723.2 92.4 %all-reduce.15.cloned.1.call-done = f32[256,256]{0,1:T(8,128)} async-done(((f32[256,256]{0,1:T(8,128)}), f32[256,256]{0,1:T(8,128)}) %all-reduce.15.cloned.1.call-update) | async-done | bytes 262160 | tf_op jit(solution)/shard_map/psum | solution.py:133
  815.6 1.1 copy.26
  816.6 1.0 fusion.8
  817.7 11.7 %cholesky.164 = f32[128,128]{1,0:T(8,128)S(1)} custom-call(f32[128,128]{1,0:T(8,128)S(1)} %cholesky.197), custom_call_target="Cholesky" | custom-call | tf_op jit(solution)/shard_map/jit(cholesky)/cholesky | solution.py:134
  829.4 9.8 custom-call.19
  839.7 11.7 %cholesky.181 = f32[128,128]{1,0:T(8,128)S(1)} custom-call(f32[128,128]{1,0:T(8,128)S(1)} %convolution_subtract_fusion.3), custom_call_target="Cholesky" | custom-call | tf_op jit(solution)/shard_map/jit(cholesky)/cholesky | solution.py:134
  851.5 0.7 compare_reduce_fusion
  854.1 4.1 while.5
  855.0 1.3 bitcast_dynamic-update-slice_fusion.5
  856.9 1.3 bitcast_dynamic-update-slice_fusion.5
  858.3 19.7 %custom-call.20 = f32[2,128,128]{1,2,0:T(8,128)S(1)} custom-call(f32[2,128,128]{2,1,0:T(8,128)S(1)} %get-tuple-element.19), custom_call_target="InvertDiagBlocksLowerTriangular" | custom-call | tf_op jit(solution)/shard_map/jit(_solve_triangular)/triangular_solve | solution.py:135
  878.8 5.6 broadcast_select_fusion
  884.4 0.8 fusion.1
  885.2 3.5 maximum_bitcast_fusion
  888.7 84.8 %all-reduce.17.cloned.1.call-done = bf16[768,256]{1,0:T(8,128)(2,1)} async-done(((bf16[768,256]{1,0:T(8,128)(2,1)}), bf16[768,256]{1,0:T(8,128)(2,1)}) %all-reduce.17.cloned.1.call-update) | async-done | bytes 393232 | tf_op jit(solution)/shard_map/psum | solution.py:25
  973.6 6.7 subtract_bitcast_fusion
  980.3 6.1 copy.28
  (117 shorter events, 13.5 us)
Async XLA Ops:
  7.2 0.7 copy-start
  24.2 113.3 %all-to-all-start = ((bf16[128,128,128]{2,1,0:T(8,128)(2,1)}), bf16[128,128,128]{2,1,0:T(8,128)(2,1)}, u32[]{:S(2)}, u32[]{:S(2)}) async-start(bf16[128,128,128]{2,1,0:T(8,128)(2,1)} %scatter_fusion), calls=%async_computation | async-start | bytes 8388608 | tf_op jit(solution)/shard_map/all_to_all | solution.py:71
  39.6 309.5 %all-reduce.21.cloned.1.call-start = ((), (), s32[]{:S(2)}) async-start(), calls=%async_computation.6 | async-start | bytes 3145728 | tf_op jit(solution)/shard_map/psum | solution.py:25
  137.5 36.4 %copy-start.4 = (bf16[12,6,128,128]{3,2,1,0:T(8,128)(2,1)S(1)}, bf16[12,6,128,128]{3,2,1,0:T(8,128)(2,1)}, u32[]{:S(2)}) copy-start(bf16[12,6,128,128]{3,2,1,0:T(8,128)(2,1)} %copy.19) | copy-start | bytes 7077892
  142.5 47.5 %collective-permute-start = (bf16[8,8,1,128,128]{4,3,1,0,2:T(8,128)(2,1)}, bf16[8,8,1,128,128]{4,3,1,0,2:T(8,128)(2,1)}, u32[]{:S(2)}, u32[]{:S(2)}) collective-permute-start(bf16[8,8,1,128,128]{4,3,1,0,2:T(8,128)(2,1)} %get-tuple-element.55), channel_id=1, source_target_pairs={{0,128},{128,0},{1,129},{129,1},{2,130},{130,2},{3,131},{131,3},{4... | collective-permute-start | bytes 6291464 | tf_op jit(solution)/shard_map/ppermute | solution.py:20
  173.9 16.0 %copy-start.5 = (bf16[1,8,8,1,128,128]{5,4,2,1,0,3:T(8,128)(2,1)S(1)}, bf16[1,8,8,1,128,128]{5,4,2,1,0,3:T(8,128)(2,1)}, u32[]{:S(2)}) copy-start(bf16[1,8,8,1,128,128]{5,4,2,1,0,3:T(8,128)(2,1)} %get-tuple-element.54) | copy-start | bytes 6291460
  238.8 2.2 copy-start.2
  242.3 202.8 %all-reduce.11.cloned.1.call-start = ((), (), s32[]{:S(2)}) async-start(), calls=%async_computation.1 | async-start | bytes 524288 | tf_op jit(solution)/shard_map/psum | solution.py:133
  349.1 1.4 copy-start.8
  350.5 1.1 copy-start.6
  352.4 249.8 %all-reduce.13.cloned.1.call-start = ((), (), s32[]{:S(2)}) async-start(), calls=%async_computation.2 | async-start | bytes 786432 | tf_op jit(solution)/shard_map/psum | solution.py:25
  513.9 205.6 %all-reduce.19.cloned.1.call-start = ((), (), s32[]{:S(2)}) async-start(), calls=%async_computation.5 | async-start | bytes 3145728 | tf_op jit(solution)/shard_map/psum | solution.py:25
  607.1 2.2 copy-start.3
  610.6 205.0 %all-reduce.15.cloned.1.call-start = ((), (), s32[]{:S(2)}) async-start(), calls=%async_computation.3 | async-start | bytes 524288 | tf_op jit(solution)/shard_map/psum | solution.py:133
  719.5 1.4 copy-start.9
  720.9 1.1 copy-start.7
  722.9 250.7 %all-reduce.17.cloned.1.call-start = ((), (), s32[]{:S(2)}) async-start(), calls=%async_computation.4 | async-start | bytes 786432 | tf_op jit(solution)/shard_map/psum | solution.py:25
  980.3 6.1 copy-start.1
Sparse Core Ops, SparseCore 0:
  242.4 106.6 all-reduce.20
  352.6 92.5 all-reduce.10
  514.0 88.1 all-reduce.12
  610.7 108.7 all-reduce.18
  723.0 92.5 all-reduce.14
  885.3 88.1 all-reduce.16
where the time goes:
time: 1000 us; the launch traced here: 994 us
  waiting for transfers between devices  669 us (67%)
  other arithmetic  156 us (16%)
  local copies, waits for them, and re-layouts  109 us (11%)
  matrix products  24.4 us (2%)
  between operations  17.8 us (2%)
  starting transfers between devices  17.1 us (2%)
    psum x4, waiting for transfers between devices, broadcast(): return lax.psum(block, axis)  389 us
    psum x2, waiting for transfers between devices, per_device(): diagonal = lax.psum(jnp.concatenate(block_rows, axis=0), 'row')  184 us
    all_to_all x1, waiting for transfers between devices, per_device(): lax.all_to_all(outgoing, ('row', 'col'), split_axis=0, concat_axis=0, til...  82.4 us
    another operation x14, other arithmetic, per_device(): lower_f = jnp.linalg.cholesky(diagonal)  69.3 us
    another operation x5, other arithmetic, per_device(): inverse = jax.scipy.linalg.solve_triangular(lower_f, identity, lower=True)  39.4 us
    scatter x1, local copies, waits for them, and re-layouts, per_device(): slot_table = jnp.full((slot_count,), spare_tile, jnp.int32).at[position.r...  30.7 us
    scatter-add x1, other arithmetic, per_device(): tile_sums = tile_sums.at[slot_table].add(received.astype(jnp.float32))  25.5 us
    unnamed x25, local copies, waits for them, and re-layouts  23.3 us
  transfers between devices with their start and end apart: 8, of which 8 were waited for; matrix products, arithmetic and copies ran while one was open for 5% of the time, Pallas kernels for 0%

commit v1 on v0

v1 whole, which is shorter than its diff:
```python
import functools

import jax
import jax.numpy as jnp
from jax import lax
from jax.experimental import pallas as pl
from jax.experimental.pallas import tpu as pltpu
from jax.sharding import Mesh
from jax.sharding import PartitionSpec as P

TILE = 128
PANEL = 256
KDIM = 512
NT = 96
NCT = 64
ROW = ("rowh", "xlo")
COL = ("z", "core")
PIECE = 8
F32 = jnp.float32
BF16 = jnp.bfloat16
HIGHEST = lax.Precision.HIGHEST


def pack_first(index, child):
    def body(index_ref, child_ref, out_ref):
        for a in range(4):
            for b in range(16):
                tile = child_ref[a * TILE : (a + 1) * TILE, b * TILE : (b + 1) * TILE]
                out_ref[index_ref[a * 16 + b]] = tile

    return pl.pallas_call(
        body,
        out_shape=jax.ShapeDtypeStruct((64, TILE, TILE), BF16),
        in_specs=[
            pl.BlockSpec(memory_space=pltpu.SMEM),
            pl.BlockSpec(memory_space=pltpu.VMEM),
        ],
        out_specs=pl.BlockSpec(memory_space=pltpu.VMEM),
        compiler_params=pltpu.CompilerParams(vmem_limit_bytes=16 << 20),
        name="pack_first",
    )(index, child)


def pack_second(index, tiles):
    def body(index_ref, tiles_ref, out_ref):
        for slot in range(64):
            out_ref[slot] = tiles_ref[index_ref[slot]]

    return pl.pallas_call(
        body,
        out_shape=jax.ShapeDtypeStruct((64, TILE, TILE), BF16),
        in_specs=[
            pl.BlockSpec(memory_space=pltpu.SMEM),
            pl.BlockSpec(memory_space=pltpu.VMEM),
        ],
        out_specs=pl.BlockSpec(memory_space=pltpu.VMEM),
        compiler_params=pltpu.CompilerParams(vmem_limit_bytes=16 << 20),
        name="pack_second",
    )(index, tiles)


def add_tiles(row_pos, col_pos, base, tiles):
    def body(row_ref, col_ref, base_ref, tiles_ref, out_ref):
        out_ref[...] = base_ref[...]
        for slot in range(64):
            rows = pl.ds(pl.multiple_of(row_ref[slot] * TILE, TILE), TILE)
            cols = pl.ds(pl.multiple_of(col_ref[slot] * TILE, TILE), TILE)
            out_ref[rows, cols] += tiles_ref[slot].astype(F32)

    return pl.pallas_call(
        body,
        out_shape=jax.ShapeDtypeStruct(base.shape, F32),
        in_specs=[
            pl.BlockSpec(memory_space=pltpu.SMEM),
            pl.BlockSpec(memory_space=pltpu.SMEM),
            pl.BlockSpec(memory_space=pltpu.VMEM),
            pl.BlockSpec(memory_space=pltpu.VMEM),
        ],
        out_specs=pl.BlockSpec(memory_space=pltpu.VMEM),
        compiler_params=pltpu.CompilerParams(vmem_limit_bytes=32 << 20),
        name="add_tiles",
    )(row_pos, col_pos, base, tiles)


def inverse_factor(diag_tiles):
    rows = []
    at = 0
    for s in range(4):
        parts = [diag_tiles[at + t] for t in range(s + 1)]
        at += s + 1
        parts += [jnp.zeros((TILE, TILE), F32)] * (3 - s)
        rows.append(jnp.concatenate(parts, axis=1))
    low = jnp.concatenate(rows, axis=0)
    full = jnp.tril(low) + jnp.tril(low, -1).T
    lower_f = jnp.linalg.cholesky(full, symmetrize_input=False)
    return jax.scipy.linalg.solve_triangular(lower_f, jnp.eye(KDIM, dtype=F32), lower=True)


def per_device(front_orig, child_update, tile_map):
    fr = lax.axis_index("front")
    r = lax.axis_index(ROW)
    c = lax.axis_index(COL)
    core = lax.axis_index("core")
    xlo = r % 2
    child_no = c // 4
    quarter = c % 4
    maps = tile_map.reshape(4, NCT)
    front = front_orig[0]

    my_cols = lax.dynamic_slice(maps, (child_no, 16 * quarter), (1, 16))[0]
    picked = []
    for s in range(4):
        hit = my_cols == s
        where_b = jnp.argmax(hit).astype(jnp.int32)
        strip = lax.dynamic_slice(child_update, (0, where_b * TILE), (4 * TILE, TILE))
        picked.append(jnp.where(jnp.any(hit), strip, jnp.zeros_like(strip)))
    picked = jnp.stack(picked).reshape(4, 4, 16, PIECE, TILE).transpose(2, 0, 1, 3, 4)
    picked = picked.reshape(16, 16 * PIECE, TILE)
    strip = front[:, :TILE].reshape(12, 16, PIECE, TILE).transpose(1, 0, 2, 3)
    strip = strip.reshape(16, 12 * PIECE, TILE)
    message = jnp.concatenate([picked, strip], axis=1)
    got = lax.all_to_all(message, COL, split_axis=0, concat_axis=0, tiled=True)
    child_piece = got[:, :128].reshape(4, 4, 128, TILE).astype(F32).sum(axis=1).astype(BF16)
    front_piece = got[:4, 128:].reshape(4, 12, PIECE, TILE)
    diag_piece = front_piece[:, 0].reshape(4 * PIECE, TILE)
    to_front = jnp.concatenate(
        [child_piece.reshape(2, 256, TILE), jnp.broadcast_to(diag_piece, (2, 32, TILE))], axis=1
    )
    message = jnp.broadcast_to(to_front[:, None], (2, 8, 288, TILE)).reshape(16, 288, TILE)
    got = lax.all_to_all(message, ("front",) + ROW, split_axis=0, concat_axis=0, tiled=True)
    blocks = got[:, :256].reshape(16, 2, 4, 4, PIECE, TILE)
    own_maps = lax.dynamic_slice(maps, (2 * fr, 0), (2, NCT))
    wanted = jnp.concatenate([r + 8 * jnp.arange(12), jnp.arange(4)])
    one_hot = (own_maps.reshape(1, 2, 16, 4) == wanted[:, None, None, None]).astype(BF16)
    added = jnp.einsum("tkna,nksapl->tspl", one_hot, blocks, preferred_element_type=F32)
    diag_front = lax.dynamic_slice(got, (8 * fr, 256, 0), (4, 32, TILE))
    front_part = jnp.concatenate(
        [front_piece.transpose(1, 0, 2, 3), diag_front.reshape(4, 4, PIECE, TILE)], axis=0
    )
    chunk = added + front_part.astype(F32)
    panel_chunk = chunk[:12].transpose(0, 2, 1, 3).reshape(12 * PIECE, KDIM)

    low_tiles = jnp.stack([chunk[12 + s, t] for s in range(4) for t in range(s + 1)])
    low_other = lax.ppermute(low_tiles, "core", [(0, 1), (1, 0)])
    first = jnp.where(core == 0, low_tiles, low_other)
    second = jnp.where(core == 0, low_other, low_tiles)
    low_pair = jnp.concatenate([first, second], axis=1)
    diag_all = lax.all_gather(low_pair, "z", axis=0)
    diag_tiles = diag_all.transpose(1, 0, 2, 3).reshape(10, TILE, TILE)
    panel_all = lax.all_gather(panel_chunk, COL, axis=0)

    inverse = inverse_factor(diag_tiles)

    a_no = jnp.arange(4)[:, None]
    x_to = (a_no // 2) ^ (quarter & 1)
    slots = (x_to * 16 + (my_cols % 16)[None, :]) * 2 + (a_no & 1)
    message = pack_first(slots.reshape(64).astype(jnp.int32), child_update)
    message = message.reshape(32, 2 * TILE, TILE)
    got = lax.all_to_all(message, ("xlo",) + COL, split_axis=0, concat_axis=0, tiled=True)
    class_of = jnp.argmax(
        (maps[:, None, :8] % 8) == jnp.arange(8)[None, :, None], axis=2
    ).astype(jnp.int32)
    kid = jnp.arange(4).reshape(2, 1, 2, 1)
    dest_row = jnp.arange(8).reshape(1, 8, 1, 1)
    half = jnp.arange(2).reshape(1, 1, 1, 2)
    klass = class_of[kid, dest_row]
    q_no = 2 * half + (((klass % 4) // 2) ^ xlo)
    source = ((klass // 4) * 16 + 4 * kid + q_no) * 2 + (klass & 1)
    message = pack_second(source.reshape(64).astype(jnp.int32), got.reshape(64, TILE, TILE))
    message = message.reshape(16, 4 * TILE, TILE)
    got = lax.all_to_all(message, ("front",) + ROW, split_axis=0, concat_axis=0, tiled=True)
    tiles = got.reshape(64, TILE, TILE)
    src_row = jnp.arange(16).reshape(16, 1, 1)
    sib = jnp.arange(2).reshape(1, 2, 1)
    half = jnp.arange(2).reshape(1, 1, 2)
    own_class = lax.dynamic_slice(class_of, (2 * fr, 0), (2, 8))[:, :]
    klass = jnp.take(own_class, r, axis=1).reshape(1, 2, 1)
    i_no = 4 * (2 * (src_row // 2) + klass // 4) + klass % 4
    q_no = 2 * half + (((klass % 4) // 2) ^ (src_row % 2))
    col_b = jnp.argmax((own_maps[:, :16] % 16) == c, axis=1).astype(jnp.int32).reshape(1, 2, 1)
    j_no = 16 * q_no + col_b
    full = (16, 2, 2)
    row_pos = own_maps[jnp.broadcast_to(sib, full), jnp.broadcast_to(i_no, full)] // 8
    col_pos = own_maps[jnp.broadcast_to(sib, full), jnp.broadcast_to(j_no, full)] // 16

    def dot_t(left, right, precision=HIGHEST):
        return lax.dot_general(
            left, right, (((1,), (1,)), ((), ())), precision=precision, preferred_element_type=F32
        )

    col_panel = jnp.arange(KDIM)[None, :] // PANEL
    g_chunk = dot_t(panel_chunk, inverse)
    chunk_t = jnp.repeat(r + 8 * jnp.arange(12), PIECE)[:, None]
    h_chunk = jnp.where(chunk_t >= 2 * (col_panel + 1), g_chunk, 0.0).astype(BF16)
    h_chunk = h_chunk.reshape(6, 2, PIECE, KDIM).transpose(1, 0, 2, 3)
    h_own = c // 8
    same = lax.dynamic_index_in_dim(h_chunk, h_own, 0, keepdims=False)
    cross = lax.dynamic_index_in_dim(h_chunk, 1 - h_own, 0, keepdims=False)
    route_same, route_cross = [], []
    for rr in range(8):
        for cc in range(16):
            h, m = cc // 8, cc % 8
            route_same.append((rr * 16 + cc, m * 16 + 8 * h + rr))
            route_cross.append((rr * 16 + cc, m * 16 + 8 * (1 - h) + rr))
    same = lax.ppermute(same, ROW + COL, route_same)
    cross = lax.ppermute(cross, ROW + COL, route_cross)
    piece = jnp.stack(
        [jnp.where(h_own == 0, same, cross), jnp.where(h_own == 0, cross, same)]
    )
    trail_cols = lax.all_gather(piece, ROW, axis=0)
    trail_cols = trail_cols.transpose(2, 1, 0, 3, 4).reshape(6 * TILE, KDIM)

    panel_rows = panel_all.reshape(16, 12, PIECE, KDIM).transpose(1, 0, 2, 3).reshape(12 * TILE, KDIM)
    row_t = jnp.repeat(r + 8 * jnp.arange(12), TILE)[:, None]
    factor = dot_t(panel_rows, inverse)
    factor = jnp.where(row_t >= 2 * col_panel, factor, 0.0)
    trail_rows = jnp.where(row_t >= 2 * (col_panel + 1), factor, 0.0)
    rows_hi = trail_rows.astype(BF16)
    rows_lo = (trail_rows - rows_hi.astype(F32)).astype(BF16)
    base = front.astype(F32) - dot_t(rows_hi, trail_cols, None) - dot_t(rows_lo, trail_cols, None)
    update = add_tiles(
        row_pos.reshape(64).astype(jnp.int32), col_pos.reshape(64).astype(jnp.int32), base, tiles
    )
    return (update[None], factor[None])


def solution(mesh):
    fine = Mesh(
        mesh.devices.reshape(2, 4, 2, 8, 2), ("front", "rowh", "xlo", "z", "core")
    )
    return jax.shard_map(
        per_device,
        mesh=fine,
        in_specs=(P("front", ROW, COL), P(("front",) + ROW, COL), P()),
        out_specs=(P("front", ROW, COL), P("front", ROW, None)),
        check_vma=False,
    )
```

time: 1000 us -> 460 us (0.46)
  waiting for transfers between devices: 669 us -> 32.9 us
  blocking collectives: 0 us -> 136 us
  local copies, waits for them, and re-layouts: 109 us -> 42.2 us
  starting transfers between devices: 17.1 us -> 38.6 us
  other arithmetic: 156 us -> 146 us
    psum x6 -> x0, waiting for transfers between devices: 573 us -> none  [the longest x4 389 us: broadcast(): return lax.psum(block, axis)]
    all_gather x0 -> x2, blocking collectives: none -> 136 us  [the longest x1 80.6 us: per_device(): diag_all = lax.all_gather(low_pair, 'z', axis=0)]
    all_to_all x1 -> x4, waiting for transfers between devices: 82.4 us -> 28.3 us  [the longest x2 18 us: per_device(): lax.all_to_all(message, ('front',) + ROW, split_axis=0, concat_axis=0, ti...]
    scatter x2 -> x0, local copies, waits for them, and re-layouts: 39.3 us -> none  [the longest x1 30.7 us: per_device(): slot_table = jnp.full((slot_count,), spare_tile, jnp.int32).at[position.r...]
    scatter-add x1 -> x0, other arithmetic: 25.5 us -> none  [per_device(): tile_sums = tile_sums.at[slot_table].add(received.astype(jnp.float32))]
    another operation x20 -> x25, other arithmetic: 111 us -> 133 us  [the longest x14 87.1 us: inverse_factor(): lower_f = jnp.linalg.cholesky(full, symmetrize_input=False)]
    unnamed x25 -> x61, local copies, waits for them, and re-layouts: 23.3 us -> 7.28 us
    all_to_all x1 -> x4, starting transfers between devices: 15.5 us -> 30.2 us  [the longest x2 14.4 us: per_device(): lax.all_to_all(message, ('front',) + ROW, split_axis=0, concat_axis=0, ti...]
  transfers between devices with their start and end apart: 8 -> 8, of which waited for: 8 -> 5; matrix products, arithmetic and copies ran while one was open for 5% -> 44% of each run, Pallas kernels for 0% -> 1%
where the time goes in v1:
time: 460 us; the launch traced here: 451 us
  other arithmetic  146 us (32%)
  blocking collectives  136 us (30%)
  local copies, waits for them, and re-layouts  42.2 us (9%)
  starting transfers between devices  38.6 us (8%)
  waiting for transfers between devices  32.9 us (7%)
  matrix products  27.7 us (6%)
  between operations  20.8 us (5%)
  Pallas kernels  6.51 us (1%)
    another operation x14, other arithmetic, inverse_factor(): lower_f = jnp.linalg.cholesky(full, symmetrize_input=False)  87.1 us
    all_gather x1, blocking collectives, per_device(): diag_all = lax.all_gather(low_pair, 'z', axis=0)  80.6 us
    all_gather x1, blocking collectives, per_device(): trail_cols = lax.all_gather(piece, ROW, axis=0)  55.7 us
    another operation x3, other arithmetic, inverse_factor(): jax.scipy.linalg.solve_triangular(lower_f, jnp.eye(KDIM, dtype=F32), lowe...  41.8 us
    all_to_all x2, waiting for transfers between devices, per_device(): lax.all_to_all(message, ('front',) + ROW, split_axis=0, concat_axis=0, ti...  18 us
    all_to_all x2, starting transfers between devices, per_device(): lax.all_to_all(message, ('front',) + ROW, split_axis=0, concat_axis=0, ti...  14.4 us
    another operation x20, local copies, waits for them, and re-layouts  14.3 us
    dot_general x4, matrix products, dot_t(): lax.dot_general(left, right, (((1,), (1,)), ((), ())), precision=precisio...  11.5 us
  transfers between devices with their start and end apart: 8, of which 5 were waited for; matrix products, arithmetic and copies ran while one was open for 44% of the time, Pallas kernels for 1%

profile of v1, /device:TPU:32, one launch (start us, length us, event | category | flops | bytes accessed | tf_op | source)
XLA Modules:
  0.0 451.4 jit_solution(17298173991980751975)
XLA Ops:
  14.1 1.0 slice.260
  15.2 3.8 dynamic-slice_select_fusion.3
  19.2 1.0 pad_maximum_fusion.1
  20.2 8.6 %all-to-all-start = ((bf16[16,224,128]{2,1,0:T(8,128)(2,1)}), bf16[16,224,128]{2,1,0:T(8,128)(2,1)S(1)}, u32[]{:S(2)}, u32[]{:S(2)}) async-start(bf16[16,224,128]{2,1,0:T(8,128)(2,1)} %pad_maximum_fusion.1), calls=%async_computation | async-start | bytes 1835008 | tf_op jit(solution)/shard_map/all_to_all | solution.py:122
  32.0 0.9 gather_fusion.1
  34.1 0.9 gather_fusion
  35.7 2.2 pack_first.1
  40.4 10.3 %all-to-all-done = bf16[16,224,128]{2,1,0:T(8,128)(2,1)S(1)} async-done(((bf16[16,224,128]{2,1,0:T(8,128)(2,1)}), bf16[16,224,128]{2,1,0:T(8,128)(2,1)S(1)}, u32[]{:S(2)}, u32[]{:S(2)}) %all-to-all-start) | async-done | bytes 917536 | tf_op jit(solution)/shard_map/all_to_all | solution.py:122
  50.8 1.2 broadcast_in_dim.97
  52.0 7.0 %all-to-all-start.1 = ((bf16[16,288,128]{2,1,0:T(8,128)(2,1)}), bf16[16,288,128]{2,1,0:T(8,128)(2,1)S(1)}, u32[]{:S(2)}, u32[]{:S(2)}) async-start(bf16[16,288,128]{2,1,0:T(8,128)(2,1)} %bitcast.22), calls=%async_computation.1 | async-start | bytes 2359296 | tf_op jit(solution)/shard_map/all_to_all | solution.py:130
  59.1 1.1 fusion.23
  61.1 18.0 %all-to-all-done.1 = bf16[16,288,128]{2,1,0:T(8,128)(2,1)S(1)} async-done(((bf16[16,288,128]{2,1,0:T(8,128)(2,1)}), bf16[16,288,128]{2,1,0:T(8,128)(2,1)S(1)}, u32[]{:S(2)}, u32[]{:S(2)}) %all-to-all-start.1) | async-done | bytes 1179680 | tf_op jit(solution)/shard_map/all_to_all | solution.py:130
  79.1 7.2 %all-to-all-start.2 = ((bf16[32,256,128]{2,1,0:T(8,128)(2,1)}), bf16[32,256,128]{2,1,0:T(8,128)(2,1)S(1)}, u32[]{:S(2)}, u32[]{:S(2)}) async-start(bf16[32,256,128]{2,1,0:T(8,128)(2,1)} %bitcast.78), calls=%async_computation.2 | async-start | bytes 4194304 | tf_op jit(solution)/shard_map/all_to_all | solution.py:159
  88.7 80.6 %all-gather = f32[80,16,128]{2,1,0:T(8,128)S(1)} all-gather(f32[10,16,128]{2,1,0:T(8,128)S(1)} %pad_maximum_fusion.6), channel_id=2, replica_groups=mesh['front'=2,'rowh'=4,'xlo'=2,'z'=8,'core'=2] {'z'}, dimensions={0}, use_global_device_ids=true | all-gather | bytes 737280 | tf_op jit(solution)/shard_map/all_gather | solution.py:148
  171.0 1.1 fusion.14
  172.1 1.6 copy.361
  173.6 1.4 bitcast_add_fusion
  175.0 1.0 copy-done.5
  176.0 11.7 %cholesky.102 = f32[128,128]{1,0:T(8,128)S(1)} custom-call(f32[128,128]{1,0:T(8,128)S(1)} %cholesky.260), custom_call_target="Cholesky" | custom-call | tf_op jit(solution)/shard_map/jit(cholesky)/cholesky | solution.py:95
  188.5 9.8 %custom-call.31 = f32[1,128,128]{1,2,0:T(8,128)S(1)} custom-call(f32[1,128,128]{2,1,0:T(8,128)S(1)} %copy.364), custom_call_target="InvertDiagBlocksLowerTriangular" | custom-call | tf_op jit(solution)/shard_map/jit(cholesky)/cholesky | solution.py:95
  198.4 1.2 fusion.29
  199.6 1.9 convolution_subtract_fusion.3
  201.5 0.8 copy.367
  202.5 0.8 cholesky.264
  203.3 11.7 %cholesky.212 = f32[128,128]{1,0:T(8,128)S(1)} custom-call(f32[128,128]{1,0:T(8,128)S(1)} %cholesky.264), custom_call_target="Cholesky" | custom-call | tf_op jit(solution)/shard_map/jit(cholesky)/cholesky | solution.py:95
  215.1 0.9 constant_dynamic-update-slice_fusion.10
  217.4 10.7 %custom-call.32 = f32[1,128,128]{1,2,0:T(8,128)S(1)} custom-call(f32[1,128,128]{2,1,0:T(8,128)} %copy.370), custom_call_target="InvertDiagBlocksLowerTriangular" | custom-call | tf_op jit(solution)/shard_map/jit(cholesky)/cholesky | solution.py:95
  228.2 1.2 convolution_dynamic-update-slice_fusion
  229.4 1.5 convolution_subtract_fusion.4
  231.6 13.2 %cholesky.233 = f32[128,128]{1,0:T(8,128)} custom-call(f32[128,128]{1,0:T(8,128)} %cholesky.269), custom_call_target="Cholesky" | custom-call | tf_op jit(solution)/shard_map/jit(cholesky)/cholesky | solution.py:95
  244.7 1.6 copy.372
  246.3 2.0 select_reduce_fusion.1
  248.3 1.6 copy.375
  249.9 11.3 %custom-call.33 = f32[1,128,128]{1,2,0:T(8,128)} custom-call(f32[1,128,128]{2,1,0:T(8,128)} %copy.375), custom_call_target="InvertDiagBlocksLowerTriangular" | custom-call | tf_op jit(solution)/shard_map/jit(cholesky)/cholesky | solution.py:95
  261.2 1.1 convolution_dynamic-update-slice_fusion.1
  262.3 1.3 convolution_subtract_fusion.5
  263.6 11.9 %cholesky.250 = f32[128,128]{1,0:T(8,128)S(1)} custom-call(f32[128,128]{1,0:T(8,128)S(1)} %convolution_subtract_fusion.5), custom_call_target="Cholesky" | custom-call | tf_op jit(solution)/shard_map/jit(cholesky)/cholesky | solution.py:95
  275.6 1.3 compare_reduce_fusion.2
  278.3 1.3 compare_reduce_fusion.1
  281.7 1.1 select_select_fusion
  283.4 14.4 %while.2 = (s32[]{:T(128)}, f32[512,512]{0,1:T(8,128)}, s32[4,2]{0,1:T(2,128)S(1)}, f32[4,128,128]{2,1,0:T(8,128)}, s32[]{:T(128)}) while((s32[]{:T(128)}, f32[512,512]{0,1:T(8,128)}, s32[4,2]{0,1:T(2,128)S(1)}, f32[4,128,128]{2,1,0:T(8,128)}, s32[]{:T(128)}) %tuple.88), condition=%wide.while_cond.1, body=%wide.while_body.1.sunk | while | flops 2 | bytes 393329 | solution.py:96
  284.0 2.3 dynamic-slice.22
  287.6 2.3 dynamic-slice.22
  291.3 2.3 dynamic-slice.22
  294.9 2.2 dynamic-slice.22
  297.8 40.1 %custom-call.34 = f32[4,128,128]{1,2,0:T(8,128)S(1)} custom-call(f32[4,128,128]{2,1,0:T(8,128)} %get-tuple-element.29), custom_call_target="InvertDiagBlocksLowerTriangular" | custom-call | tf_op jit(solution)/shard_map/jit(_solve_triangular)/triangular_solve | solution.py:96
  337.9 1.1 fusion.25
  339.0 1.4 convolution_subtract_fusion.1
  340.9 1.5 convolution_subtract_fusion
  342.8 1.8 convolution_subtract_fusion.2
  345.1 1.1 fusion.10
  346.3 2.8 collective-permute-start.1
  349.0 5.4 %collective-permute-start.2 = (bf16[6,8,512]{2,1,0:T(8,128)(2,1)S(1)}, bf16[6,8,512]{2,1,0:T(8,128)(2,1)S(1)}, u32[]{:S(2)}, u32[]{:S(2)}) collective-permute-start(bf16[6,8,512]{2,1,0:T(8,128)(2,1)S(1)} %get-tuple-element.110), channel_id=1, source_target_pairs={{0,8},{1,24},{2,40},{3,56},{4,72},{5,88},{6,104},{7,120},{8,0},{9,... | collective-permute-start | bytes 147464 | tf_op jit(solution)/shard_map/ppermute | solution.py:206
  354.9 3.9 collective-permute-done.2
  359.5 1.4 copy-done.1
  360.9 7.4 %all-to-all-start.3 = ((bf16[16,512,128]{2,1,0:T(8,128)(2,1)}), bf16[16,512,128]{2,1,0:T(8,128)(2,1)S(1)}, u32[]{:S(2)}, u32[]{:S(2)}) async-start(bf16[16,512,128]{2,1,0:T(8,128)(2,1)} %bitcast.184), calls=%async_computation.3 | async-start | bytes 4194304 | tf_op jit(solution)/shard_map/all_to_all | solution.py:171
  368.3 55.7 %all-gather.1 = bf16[16,6,8,512]{3,2,1,0:T(8,128)(2,1)S(1)} all-gather(bf16[2,6,8,512]{3,2,1,0:T(8,128)(2,1)S(1)} %pad_maximum_fusion.5), channel_id=3, replica_groups=mesh['front'=2,'rowh'=4,'xlo'=2,'z'=8,'core'=2] {'rowh','xlo'}, dimensions={0}, use_global_device_ids=true | all-gather | bytes 884736 | tf_op jit(solution)/shard_map/all_gather | solution.py:210
  424.1 2.3 copy.341
  426.4 5.5 %convolution_select_fusion = f32[1536,512]{1,0:T(8,128)S(1)} fusion(f32[1536,512]{1,0:T(8,128)S(1)} %bitcast.187, s32[512]{0:T(512)S(1)} %fusion.64, s32[1536]{0:T(1024)S(1)} %broadcast_bitcast_fusion, f32[128,512]{1,0:T(8,128)S(1)} %copy-done.9, f32[128,512]{1,0:T(8,128)S(1)} %copy-done.7, f32[128,512]{1,0:T(8,128)S(1)} %fusion.39, f32[128,512]{1,0:T(8,128)S(1)} %fusion.25), kind=kOutput, calls=%fused_computation.6 | convolution fusion | flops 4834197504 | bytes 7348224 | tf_op jit(solution)/shard_map/dot_general | solution.py:187
  432.0 1.4 fusion.1
  433.6 1.2 copy-done.4
  434.8 3.4 subtract_subtract_fusion.base_ref
  438.2 2.3 copy-done
  440.6 3.6 add_tiles.1
  (188 shorter events, 29.4 us)
Async XLA Ops:
  18.9 9.8 %copy-start.24 = (s32[2,2,64]{2,1,0:T(2,128)S(1)}, s32[2,2,64]{2,1,0:T(2,128)}, u32[]{:S(2)}) copy-start(s32[2,2,64]{2,1,0:T(2,128)} %param.5) | copy-start | bytes 3076
  20.2 30.5 %all-to-all-start = ((bf16[16,224,128]{2,1,0:T(8,128)(2,1)}), bf16[16,224,128]{2,1,0:T(8,128)(2,1)S(1)}, u32[]{:S(2)}, u32[]{:S(2)}) async-start(bf16[16,224,128]{2,1,0:T(8,128)(2,1)} %pad_maximum_fusion.1), calls=%async_computation | async-start | bytes 1835008 | tf_op jit(solution)/shard_map/all_to_all | solution.py:122
  34.1 1.6 copy-start.2
  52.0 27.1 %all-to-all-start.1 = ((bf16[16,288,128]{2,1,0:T(8,128)(2,1)}), bf16[16,288,128]{2,1,0:T(8,128)(2,1)S(1)}, u32[]{:S(2)}, u32[]{:S(2)}) async-start(bf16[16,288,128]{2,1,0:T(8,128)(2,1)} %bitcast.22), calls=%async_computation.1 | async-start | bytes 2359296 | tf_op jit(solution)/shard_map/all_to_all | solution.py:130
  79.1 279.8 %all-to-all-start.2 = ((bf16[32,256,128]{2,1,0:T(8,128)(2,1)}), bf16[32,256,128]{2,1,0:T(8,128)(2,1)S(1)}, u32[]{:S(2)}, u32[]{:S(2)}) async-start(bf16[32,256,128]{2,1,0:T(8,128)(2,1)} %bitcast.78), calls=%async_computation.2 | async-start | bytes 4194304 | tf_op jit(solution)/shard_map/all_to_all | solution.py:159
  86.2 337.9 %all-gather.4.cloned.1.call-start = ((), (), s32[]{:S(2)}) async-start(), calls=%async_computation.4 | async-start | bytes 3342336 | tf_op jit(solution)/shard_map/all_gather | solution.py:150
  87.3 1.3 collective-permute-start
  169.4 1.0 copy-start.10
  169.5 0.9 copy-start.11
  169.6 0.8 copy-start.12
  169.7 0.7 copy-start.13
  169.8 0.6 copy-start.14
  169.9 0.6 copy-start.15
  170.0 0.6 copy-start.16
  170.1 0.6 copy-start.17
  170.3 0.6 copy-start.18
  170.4 0.6 copy-start.19
  170.4 0.6 copy-start.20
  175.0 1.0 copy-start.5
  297.8 47.3 %copy-start.22 = (s32[512]{0:T(512)S(1)}, s32[512]{0:T(512)}, u32[]{:S(2)}) copy-start(s32[512]{0:T(512)} %fusion.66) | copy-start | bytes 6148
  297.8 47.3 %copy-start.25 = (s32[96]{0:T(128)S(1)}, s32[96]{0:T(128)}, u32[]{:S(2)}) copy-start(s32[96]{0:T(128)} %ge.61) | copy-start | bytes 1156
  340.9 13.6 %copy-start.21 = (s32[2,8,2,2]{3,2,1,0:T(2,128)S(1)}, s32[2,8,2,2]{3,2,1,0:T(2,128)}, u32[]{:S(2)}) copy-start(s32[2,8,2,2]{3,2,1,0:T(2,128)} %multiply_add_fusion) | copy-start | bytes 772
  342.8 2.3 copy-start.6
  345.1 1.2 copy-start.8
  346.3 8.7 %collective-permute-start.1 = (bf16[6,8,512]{2,1,0:T(8,128)(2,1)S(1)}, bf16[6,8,512]{2,1,0:T(8,128)(2,1)S(1)}, u32[]{:S(2)}, u32[]{:S(2)}) collective-permute-start(bf16[6,8,512]{2,1,0:T(8,128)(2,1)S(1)} %get-tuple-element.109), channel_id=1, source_target_pairs={{0,0},{1,16},{2,32},{3,48},{4,64},{5,80},{6,96},{7,112},{8,8},{9,2... | collective-permute-start | bytes 147464 | tf_op jit(solution)/shard_map/ppermute | solution.py:205
  349.0 9.8 %collective-permute-start.2 = (bf16[6,8,512]{2,1,0:T(8,128)(2,1)S(1)}, bf16[6,8,512]{2,1,0:T(8,128)(2,1)S(1)}, u32[]{:S(2)}, u32[]{:S(2)}) collective-permute-start(bf16[6,8,512]{2,1,0:T(8,128)(2,1)S(1)} %get-tuple-element.110), channel_id=1, source_target_pairs={{0,8},{1,24},{2,40},{3,56},{4,72},{5,88},{6,104},{7,120},{8,0},{9,... | collective-permute-start | bytes 147464 | tf_op jit(solution)/shard_map/ppermute | solution.py:206
  359.5 1.4 copy-start.1
  360.9 77.3 %all-to-all-start.3 = ((bf16[16,512,128]{2,1,0:T(8,128)(2,1)}), bf16[16,512,128]{2,1,0:T(8,128)(2,1)S(1)}, u32[]{:S(2)}, u32[]{:S(2)}) async-start(bf16[16,512,128]{2,1,0:T(8,128)(2,1)} %bitcast.184), calls=%async_computation.3 | async-start | bytes 4194304 | tf_op jit(solution)/shard_map/all_to_all | solution.py:171
  424.1 2.3 copy-start.7
  424.1 2.3 copy-start.9
  426.4 5.6 %copy-start.23 = (s32[512]{0:T(512)S(1)}, s32[512]{0:T(512)}, u32[]{:S(2)}) copy-start(s32[512]{0:T(512)} %fusion.66) | copy-start | bytes 6148
  432.0 1.7 copy-start.3
  432.0 2.8 copy-start.4
  438.2 2.3 copy-start
Sparse Core Ops, SparseCore 0:
  88.9 61.9 all-gather.3

commit v2 on v1

v2 whole, which is shorter than its diff:
```python
import functools

import jax
import jax.numpy as jnp
from jax import lax
from jax.experimental import pallas as pl
from jax.experimental.pallas import tpu as pltpu
from jax.sharding import Mesh
from jax.sharding import PartitionSpec as P

TILE = 128
PANEL = 256
KDIM = 512
NT = 96
NCT = 64
ROW = ("rowh", "xlo")
COL = ("z", "core")
PIECE = 8
F32 = jnp.float32
BF16 = jnp.bfloat16


def pack_first(place, maps, child, front):
    def body(place_ref, maps_ref, child_ref, front_ref, panel_ref, tiles_ref):
        child_no, quarter = place_ref[0], place_ref[1]
        targets = [maps_ref[child_no, 16 * quarter + b] for b in range(16)]

        def spread(block, at, count):
            for c in range(16):
                for n in range(0, count, 2):
                    pair = [block[m * TILE + 8 * c : m * TILE + 8 * c + 8] for m in (n, n + 1)]
                    panel_ref[c, at + 8 * n : at + 8 * n + 16, :] = jnp.concatenate(
                        pair, axis=0
                    ).astype(BF16)

        for s in range(4):
            found = jnp.int32(-1)
            for b in range(16):
                found = jnp.where(targets[b] == s, b, found)
            start = pl.multiple_of(jnp.maximum(found, 0) * TILE, TILE)
            strip = child_ref[:, pl.ds(start, TILE)].astype(F32)
            spread(jnp.where(found >= 0, strip, 0.0), 32 * s, 4)
        spread(front_ref[...].astype(F32), 128, 12)
        for b in range(16):
            col = targets[b] % 16
            for a in range(4):
                to = ((a // 2) ^ (quarter % 2)) * 32 + col * 2 + a % 2
                tile = child_ref[a * TILE : (a + 1) * TILE, b * TILE : (b + 1) * TILE]
                tiles_ref[to] = tile

    smem = pl.BlockSpec(memory_space=pltpu.SMEM)
    return pl.pallas_call(
        body,
        grid=(1,),
        out_shape=[
            jax.ShapeDtypeStruct((16, 224, TILE), BF16),
            jax.ShapeDtypeStruct((64, TILE, TILE), BF16),
        ],
        in_specs=[
            smem,
            smem,
            pl.BlockSpec(child.shape, lambda i: (0, 0)),
            pl.BlockSpec((12 * TILE, TILE), lambda i: (0, 0)),
        ],
        out_specs=[
            pl.BlockSpec((16, 224, TILE), lambda i: (0, 0, 0)),
            pl.BlockSpec((64, TILE, TILE), lambda i: (0, 0, 0)),
        ],
        compiler_params=pltpu.CompilerParams(vmem_limit_bytes=32 << 20),
        name="pack_first",
    )(place, maps, child, front)


def pack_second(index, tiles):
    def body(index_ref, tiles_ref, out_ref):
        for slot in range(64):
            out_ref[slot] = tiles_ref[index_ref[slot]]

    return pl.pallas_call(
        body,
        out_shape=jax.ShapeDtypeStruct((64, TILE, TILE), BF16),
        in_specs=[
            pl.BlockSpec(memory_space=pltpu.SMEM),
            pl.BlockSpec(memory_space=pltpu.VMEM),
        ],
        out_specs=pl.BlockSpec(memory_space=pltpu.VMEM),
        compiler_params=pltpu.CompilerParams(vmem_limit_bytes=16 << 20),
        name="pack_second",
    )(index, tiles)


def split_dot(left, right, dims):
    l_hi = left.astype(BF16)
    l_lo = (left - l_hi.astype(F32)).astype(BF16)
    r_hi = right.astype(BF16)
    r_lo = (right - r_hi.astype(F32)).astype(BF16)
    dot = functools.partial(
        lax.dot_general, dimension_numbers=(dims, ((), ())), preferred_element_type=F32
    )
    return dot(l_hi, r_hi) + (dot(l_hi, r_lo) + dot(l_lo, r_hi))


def inverse_factor(gathered):
    def body(piece_ref, w_ref, big, small):
        lane = lax.broadcasted_iota(jnp.int32, (TILE, 2 * KDIM), 1)
        sub8 = lax.broadcasted_iota(jnp.int32, (8, 2 * TILE), 0)
        for s in range(4):
            for piece in range(16):
                at = s * TILE + piece * 8
                for t in range(4):
                    row = (s * 4 + t) * 8
                    big[at : at + 8, t * TILE : (t + 1) * TILE] = piece_ref[piece, row : row + 8, :]
        row_no = lax.broadcasted_iota(jnp.int32, (KDIM, KDIM), 0)
        col_no = lax.broadcasted_iota(jnp.int32, (KDIM, KDIM), 1)
        big[:, KDIM:] = (row_no == col_no).astype(F32)
        eye = (
            lax.broadcasted_iota(jnp.int32, (TILE, TILE), 0)
            == lax.broadcasted_iota(jnp.int32, (TILE, TILE), 1)
        ).astype(F32)

        def block(j, carry):
            start = pl.multiple_of(j * TILE, TILE)
            rows = pl.ds(start, TILE)
            small[:, :TILE] = big[rows, pl.ds(start, TILE)]
            small[:, TILE:] = eye
            for b in range(TILE // 8):
                lo = 8 * b
                panel = small[lo : lo + 8, :]
                cols = [
                    jnp.broadcast_to(panel[:, lo + m : lo + m + 1], (8, TILE)) for m in range(8)
                ]
                for m in range(8):
                    pivot = jnp.broadcast_to(cols[m][m : m + 1], (8, TILE))
                    inv = lax.rsqrt(pivot)
                    inv = inv * (1.5 - 0.5 * pivot * inv * inv)
                    low = cols[m] * inv
                    for n in range(m + 1, 8):
                        cols[n] = cols[n] - low * (
                            jnp.broadcast_to(cols[n][m : m + 1], (8, TILE)) * inv
                        )
                    inv2 = jnp.concatenate([inv, inv], axis=1)
                    low2 = jnp.concatenate([low, low], axis=1)
                    scaled = jnp.broadcast_to(panel[m : m + 1], (8, 2 * TILE)) * inv2
                    panel = jnp.where(
                        sub8 > m, panel - low2 * scaled, jnp.where(sub8 == m, scaled, panel)
                    )
                small[lo : lo + 8, :] = panel
                if b < TILE // 8 - 1:
                    hi = panel.astype(BF16).astype(F32)
                    rest = panel - hi
                    left = jnp.concatenate([hi, hi, rest], axis=0)[:, :TILE].astype(BF16)
                    right = jnp.concatenate([hi, rest, hi], axis=0).astype(BF16)
                    change = lax.dot_general(
                        left, right, (((0,), (0,)), ((), ())), preferred_element_type=F32
                    )
                    small[lo + 8 :, :] = small[lo + 8 :, :] - change[lo + 8 :, :]
            upper = split_dot(small[:, TILE:], big[rows, :], ((1,), (0,)))
            big[rows, :] = upper
            below = jnp.where(lane >= start + TILE, upper, 0.0)[:, :KDIM]
            big[...] = big[...] - split_dot(below, upper, ((0,), (0,)))
            return carry

        lax.fori_loop(0, 4, block, 0)
        w_ref[...] = jnp.where(row_no >= col_no, big[:, KDIM:], 0.0)

    return pl.pallas_call(
        body,
        grid=(1,),
        out_shape=jax.ShapeDtypeStruct((KDIM, KDIM), F32),
        in_specs=[pl.BlockSpec((16, TILE, TILE), lambda i: (0, 0, 0))],
        out_specs=pl.BlockSpec((KDIM, KDIM), lambda i: (0, 0)),
        scratch_shapes=[
            pltpu.VMEM((KDIM, 2 * KDIM), F32),
            pltpu.VMEM((TILE, 2 * TILE), F32),
        ],
        compiler_params=pltpu.CompilerParams(vmem_limit_bytes=24 << 20),
        name="inverse_factor",
    )(gathered)


def solve_rows(first_tile, gathered, inverse):
    def body(tile_ref, piece_ref, w_ref, g_ref, hi_ref, lo_ref, rows, w_hi, w_lo):
        lt = pl.program_id(0)

        @pl.when(lt == 0)
        def _():
            hi = w_ref[...].astype(BF16)
            w_hi[...] = hi
            w_lo[...] = (w_ref[...] - hi.astype(F32)).astype(BF16)

        for piece in range(16):
            for s in range(4):
                rows[piece * 8 : piece * 8 + 8, s * TILE : (s + 1) * TILE] = piece_ref[
                    piece, s * 8 : s * 8 + 8, :
                ]
        f_hi = rows[...].astype(BF16)
        f_lo = (rows[...] - f_hi.astype(F32)).astype(BF16)
        dot = functools.partial(
            lax.dot_general,
            dimension_numbers=(((1,), (1,)), ((), ())),
            preferred_element_type=F32,
        )
        g = dot(f_hi, w_hi[...]) + (dot(f_hi, w_lo[...]) + dot(f_lo, w_hi[...]))
        tile_no = tile_ref[0] + 8 * lt
        panel_no = lax.broadcasted_iota(jnp.int32, (TILE, KDIM), 1) // PANEL
        g = jnp.where(tile_no >= 2 * panel_no, g, 0.0)
        g_ref[...] = g
        h = jnp.where(tile_no >= 2 * panel_no + 2, g, 0.0)
        h_hi = h.astype(BF16)
        hi_ref[...] = h_hi
        lo_ref[...] = (h - h_hi.astype(F32)).astype(BF16)

    rows_spec = pl.BlockSpec((TILE, KDIM), lambda lt, tile: (lt, 0))
    return pl.pallas_call(
        body,
        grid_spec=pltpu.PrefetchScalarGridSpec(
            num_scalar_prefetch=1,
            grid=(12,),
            in_specs=[
                pl.BlockSpec((16, 32, TILE), lambda lt, tile: (0, lt, 0)),
                pl.BlockSpec((KDIM, KDIM), lambda lt, tile: (0, 0)),
            ],
            out_specs=[rows_spec, rows_spec, rows_spec],
            scratch_shapes=[
                pltpu.VMEM((TILE, KDIM), F32),
                pltpu.VMEM((KDIM, KDIM), BF16),
                pltpu.VMEM((KDIM, KDIM), BF16),
            ],
        ),
        out_shape=[
            jax.ShapeDtypeStruct((12 * TILE, KDIM), F32),
            jax.ShapeDtypeStruct((12 * TILE, KDIM), BF16),
            jax.ShapeDtypeStruct((12 * TILE, KDIM), BF16),
        ],
        compiler_params=pltpu.CompilerParams(vmem_limit_bytes=24 << 20),
        name="solve_rows",
    )(first_tile, gathered, inverse)


def trailing_update(front, rows_hi, rows_lo, trail):
    def body(front_ref, hi_ref, lo_ref, trail_ref, out_ref, cols):
        @pl.when(pl.program_id(0) == 0)
        def _():
            for j in range(6):
                for p in range(0, 8, 2):
                    one = trail_ref[p, 16 * j : 16 * j + 16, :].astype(F32)
                    two = trail_ref[p + 1, 16 * j : 16 * j + 16, :].astype(F32)
                    for h in range(2):
                        at = j * TILE + 64 * h + 8 * p
                        both = jnp.concatenate(
                            [one[8 * h : 8 * h + 8], two[8 * h : 8 * h + 8]], axis=0
                        )
                        cols[at : at + 16, :] = both.astype(BF16)

        dot = functools.partial(
            lax.dot_general,
            dimension_numbers=(((1,), (1,)), ((), ())),
            preferred_element_type=F32,
        )
        out_ref[...] = front_ref[...].astype(F32) - (
            dot(hi_ref[...], cols[...]) + dot(lo_ref[...], cols[...])
        )

    width = front.shape[1]
    return pl.pallas_call(
        body,
        grid=(6,),
        in_specs=[
            pl.BlockSpec((2 * TILE, width), lambda n: (n, 0)),
            pl.BlockSpec((2 * TILE, KDIM), lambda n: (n, 0)),
            pl.BlockSpec((2 * TILE, KDIM), lambda n: (n, 0)),
            pl.BlockSpec((8, 96, KDIM), lambda n: (0, 0, 0)),
        ],
        out_specs=pl.BlockSpec((2 * TILE, width), lambda n: (n, 0)),
        scratch_shapes=[pltpu.VMEM((6 * TILE, KDIM), BF16)],
        out_shape=jax.ShapeDtypeStruct(front.shape, F32),
        compiler_params=pltpu.CompilerParams(vmem_limit_bytes=24 << 20),
        name="trailing_update",
    )(front, rows_hi, rows_lo, trail)


def add_tiles(tile_at, col_at, base, tiles):
    def body(at_ref, col_ref, base_ref, tiles_ref, out_ref):
        lt = pl.program_id(0)
        out_ref[...] = base_ref[...]
        for n in range(8):
            source = at_ref[lt * 8 + n]

            @pl.when(source >= 0)
            def _():
                where_col = pl.multiple_of(col_ref[lt * 8 + n] * TILE, TILE)
                out_ref[:, pl.ds(where_col, TILE)] += tiles_ref[source].astype(F32)

    width = base.shape[1]
    return pl.pallas_call(
        body,
        grid_spec=pltpu.PrefetchScalarGridSpec(
            num_scalar_prefetch=2,
            grid=(12,),
            in_specs=[
                pl.BlockSpec((TILE, width), lambda lt, a, b: (lt, 0)),
                pl.BlockSpec((64, TILE, TILE), lambda lt, a, b: (0, 0, 0)),
            ],
            out_specs=pl.BlockSpec((TILE, width), lambda lt, a, b: (lt, 0)),
        ),
        out_shape=jax.ShapeDtypeStruct(base.shape, F32),
        compiler_params=pltpu.CompilerParams(vmem_limit_bytes=24 << 20),
        name="add_tiles",
    )(tile_at, col_at, base, tiles)


def per_device(front_orig, child_update, tile_map):
    fr = lax.axis_index("front")
    r = lax.axis_index(ROW)
    c = lax.axis_index(COL)
    xlo = r % 2
    child_no = c // 4
    quarter = c % 4
    maps = tile_map.reshape(4, NCT)
    front = front_orig[0]

    place = jnp.stack([child_no, quarter]).astype(jnp.int32)
    message, first_tiles = pack_first(place, maps, child_update, front)
    got = lax.all_to_all(message, COL, split_axis=0, concat_axis=0, tiled=True)
    child_piece = got[:, :128].reshape(4, 4, 128, TILE).astype(F32).sum(axis=1).astype(BF16)
    front_piece = got[:4, 128:].reshape(4, 12, PIECE, TILE)
    diag_piece = front_piece[:, 0].reshape(4 * PIECE, TILE)
    to_front = jnp.concatenate(
        [child_piece.reshape(2, 256, TILE), jnp.broadcast_to(diag_piece, (2, 32, TILE))], axis=1
    )
    message = jnp.broadcast_to(to_front[:, None], (2, 8, 288, TILE)).reshape(16, 288, TILE)
    got = lax.all_to_all(message, ("front",) + ROW, split_axis=0, concat_axis=0, tiled=True)
    blocks = got[:, :256].reshape(16, 2, 4, 4, PIECE, TILE)
    own_maps = lax.dynamic_slice(maps, (2 * fr, 0), (2, NCT))
    wanted = jnp.concatenate([r + 8 * jnp.arange(12), jnp.arange(4)])
    one_hot = (own_maps.reshape(1, 2, 16, 4) == wanted[:, None, None, None]).astype(BF16)
    added = jnp.einsum("tkna,nksapl->tspl", one_hot, blocks, preferred_element_type=F32)
    diag_front = lax.dynamic_slice(got, (8 * fr, 256, 0), (4, 32, TILE))
    front_part = jnp.concatenate(
        [front_piece.transpose(1, 0, 2, 3), diag_front.reshape(4, 4, PIECE, TILE)], axis=0
    )
    chunk = added + front_part.astype(F32)
    diag_all = lax.all_gather(chunk[12:].reshape(128, TILE), COL, axis=0)
    panel_all = lax.all_gather(chunk[:12].reshape(384, TILE), COL, axis=0)
    inverse = inverse_factor(diag_all)

    panel_chunk = chunk[:12].transpose(0, 2, 1, 3).reshape(12 * PIECE, KDIM)
    g_chunk = lax.dot_general(
        panel_chunk,
        inverse,
        (((1,), (1,)), ((), ())),
        precision=lax.Precision.HIGHEST,
        preferred_element_type=F32,
    )
    chunk_t = jnp.repeat(r + 8 * jnp.arange(12), PIECE)[:, None]
    after = 2 * (jnp.arange(KDIM)[None, :] // PANEL) + 2
    h_chunk = jnp.where(chunk_t >= after, g_chunk, 0.0).astype(BF16)
    h_chunk = h_chunk.reshape(6, 2, PIECE, KDIM).transpose(1, 0, 2, 3)
    h_own = c // 8
    same = lax.dynamic_index_in_dim(h_chunk, h_own, 0, keepdims=False)
    cross = lax.dynamic_index_in_dim(h_chunk, 1 - h_own, 0, keepdims=False)
    route_same, route_cross = [], []
    for rr in range(8):
        for cc in range(16):
            h, m = cc // 8, cc % 8
            route_same.append((rr * 16 + cc, m * 16 + 8 * h + rr))
            route_cross.append((rr * 16 + cc, m * 16 + 8 * (1 - h) + rr))
    same = lax.ppermute(same, ROW + COL, route_same)
    cross = lax.ppermute(cross, ROW + COL, route_cross)
    first = jnp.where(h_own == 0, same, cross)
    second = jnp.where(h_own == 0, cross, same)
    piece = jnp.concatenate([first, second], axis=1).reshape(96, KDIM)
    trail = lax.all_to_all(
        jnp.broadcast_to(piece, (8, 96, KDIM)), ROW, split_axis=0, concat_axis=0, tiled=True
    )

    message = first_tiles.reshape(32, 2 * TILE, TILE)
    got = lax.all_to_all(message, ("xlo",) + COL, split_axis=0, concat_axis=0, tiled=True)
    got, trail = lax.optimization_barrier((got, trail))
    class_of = jnp.argmax(
        (maps[:, None, :8] % 8) == jnp.arange(8)[None, :, None], axis=2
    ).astype(jnp.int32)
    kid = jnp.arange(4).reshape(2, 1, 2, 1)
    dest_row = jnp.arange(8).reshape(1, 8, 1, 1)
    half = jnp.arange(2).reshape(1, 1, 1, 2)
    klass = class_of[kid, dest_row]
    q_no = 2 * half + (((klass % 4) // 2) ^ xlo)
    source = ((klass // 4) * 16 + 4 * kid + q_no) * 2 + (klass & 1)
    message = pack_second(source.reshape(64).astype(jnp.int32), got.reshape(64, TILE, TILE))
    message = message.reshape(16, 4 * TILE, TILE)
    got = lax.all_to_all(message, ("front",) + ROW, split_axis=0, concat_axis=0, tiled=True)
    tiles = got.reshape(64, TILE, TILE)
    match = own_maps[None] == (r + 8 * jnp.arange(12))[:, None, None]
    i_no = jnp.argmax(match, axis=2).astype(jnp.int32)[:, :, None, None]
    present = jnp.any(match, axis=2)[:, :, None, None]
    sib = jnp.arange(2).reshape(1, 2, 1, 1)
    x_from = jnp.arange(2).reshape(1, 1, 2, 1)
    half = jnp.arange(2).reshape(1, 1, 1, 2)
    sender = (i_no // 32) * 8 + (i_no % 32) // 8 * 2 + x_from
    tile_at = jnp.where(present, (sender * 2 + sib) * 2 + half, -1)
    col_b = jnp.argmax((own_maps[:, :16] % 16) == c, axis=1).astype(jnp.int32)
    col_tiles = own_maps.reshape(2, 4, 16)
    col_tiles = jnp.take_along_axis(col_tiles, col_b.reshape(2, 1, 1), axis=2)[:, :, 0] // 16
    q_no = 2 * half + (((i_no % 4) // 2) ^ x_from)
    col_at = jnp.zeros(q_no.shape[:1] + (2, 2, 2), jnp.int32)
    for q in range(4):
        col_at = jnp.where(q_no == q, col_tiles[:, q].reshape(1, 2, 1, 1), col_at)

    factor, rows_hi, rows_lo = solve_rows(r.reshape(1).astype(jnp.int32), panel_all, inverse)
    base = trailing_update(front, rows_hi, rows_lo, trail)
    update = add_tiles(
        tile_at.reshape(96).astype(jnp.int32), col_at.reshape(96).astype(jnp.int32), base, tiles
    )
    return (update[None], factor[None])


def solution(mesh):
    fine = Mesh(
        mesh.devices.reshape(2, 4, 2, 8, 2), ("front", "rowh", "xlo", "z", "core")
    )
    return jax.shard_map(
        per_device,
        mesh=fine,
        in_specs=(P("front", ROW, COL), P(("front",) + ROW, COL), P()),
        out_specs=(P("front", ROW, COL), P("front", ROW, None)),
        check_vma=False,
    )
```

time: 460 us -> 245 us (0.53); the launches traced: 451 us -> 244 us
  other arithmetic: 146 us -> 3.98 us
  blocking collectives: 136 us -> 31.5 us
  waiting for transfers between devices: 32.9 us -> 87.2 us
  Pallas kernels: 6.51 us -> 52.2 us
  matrix products: 27.7 us -> 1.88 us
  local copies, waits for them, and re-layouts: 42.2 us -> 19.5 us
  between operations: 20.8 us -> 14.5 us
  starting transfers between devices: 38.6 us -> 33.6 us
    all_gather x2 -> x0, blocking collectives: 136 us -> none  [the longest x1 80.6 us: per_device(): diag_all = lax.all_gather(low_pair, 'z', axis=0)]
    another operation x24 -> x3, other arithmetic: 132 us -> 1.86 us  [the longest x1 1.18 us: per_device(): i_no = jnp.argmax(match, axis=2).astype(jnp.int32)[:, :, None, None]]
    pallas_call x2 -> x5, Pallas kernels: 5.83 us -> 51.6 us  [the longest x1 30.3 us: inverse_factor(): pl.pallas_call(body, grid=(1,), out_shape=jax.ShapeDtypeStruct((KDIM, KDI...]
    all_gather x1 -> x2, waiting for transfers between devices: 0.02 us -> 32.8 us  [the longest x1 32.8 us: per_device(): diag_all = lax.all_gather(chunk[12:].reshape(128, TILE), COL, axis=0)]
    all_to_all x0 -> x1, blocking collectives: none -> 31.5 us  [per_device(): got = lax.all_to_all(message, COL, split_axis=0, concat_axis=0, tiled=True)]
    another operation x35 -> x0, local copies, waits for them, and re-layouts: 22.5 us -> none
    another operation x13 -> x0, matrix products: 15.4 us -> none  [the longest x6 8.35 us: inverse_factor(): lower_f = jnp.linalg.cholesky(full, symmetrize_input=False)]
    all_to_all x2, waiting for transfers between devices: 18 us -> 31.4 us  [per_device(): lax.all_to_all(message, ('front',) + ROW, split_axis=0, concat_axis=0, ti...]
  transfers between devices with their start and end apart: 8 -> 8, of which waited for: 5 -> 6; matrix products, arithmetic and copies ran while one was open for 44% -> 4% of each run, Pallas kernels for 1% -> 18%
where the time goes in v2:
time: 245 us; the launch traced here: 244 us
  waiting for transfers between devices  87.2 us (36%)
  Pallas kernels  52.2 us (21%)
  starting transfers between devices  33.6 us (14%)
  blocking collectives  31.5 us (13%)
  local copies, waits for them, and re-layouts  19.5 us (8%)
  between operations  14.5 us (6%)
  other arithmetic  3.98 us (2%)
    all_gather x1, waiting for transfers between devices, per_device(): diag_all = lax.all_gather(chunk[12:].reshape(128, TILE), COL, axis=0)  32.8 us
    all_to_all x1, blocking collectives, per_device(): got = lax.all_to_all(message, COL, split_axis=0, concat_axis=0, tiled=True)  31.5 us
    all_to_all x2, waiting for transfers between devices, per_device(): lax.all_to_all(message, ('front',) + ROW, split_axis=0, concat_axis=0, ti...  31.4 us
    pallas_call x1, Pallas kernels, inverse_factor(): pl.pallas_call(body, grid=(1,), out_shape=jax.ShapeDtypeStruct((KDIM, KDI...  30.3 us
    all_to_all x1, waiting for transfers between devices, per_device(): lax.all_to_all(jnp.broadcast_to(piece, (8, 96, KDIM)), ROW, split_axis=0,...  13.3 us
    unnamed x23, local copies, waits for them, and re-layouts  12.9 us
    all_to_all x2, starting transfers between devices, per_device(): lax.all_to_all(message, ('front',) + ROW, split_axis=0, concat_axis=0, ti...  10.8 us
    ppermute x1, starting transfers between devices, per_device(): same = lax.ppermute(same, ROW + COL, route_same)  9.92 us
  transfers between devices with their start and end apart: 8, of which 6 were waited for; matrix products, arithmetic and copies ran while one was open for 4% of the time, Pallas kernels for 18%

profile of v2, /device:TPU:32, one launch (start us, length us, event | category | flops | bytes accessed | tf_op | source)
XLA Modules:
  0.0 244.5 jit_solution(1388121724437658191)
XLA Ops:
  7.2 0.1 pad_add_fusion.2.place_ref
  7.3 1.7 copy-done.2
  8.9 1.6 copy-done.6
  10.5 0.7 copy-done.9
  11.2 1.2 pack_first.1
  12.5 31.5 %all_to_all.25 = bf16[16,224,128]{2,1,0:T(8,128)(2,1)S(1)} all-to-all(bf16[16,224,128]{2,1,0:T(8,128)(2,1)S(1)} %get-tuple-element.14), channel_id=1, replica_groups=mesh['front'=2,'rowh'=4,'xlo'=2,'z'=8,'core'=2] {'z','core'}, dimensions={0} | all-to-all | bytes 1835008 | tf_op jit(solution)/shard_map/all_to_all | solution.py:324
  44.0 0.1 bitcast_reduce_fusion
  44.2 1.2 broadcast_in_dim.108
  45.3 7.0 %all-to-all-start.1 = ((bf16[16,288,128]{2,1,0:T(8,128)(2,1)}), bf16[16,288,128]{2,1,0:T(8,128)(2,1)S(1)}, u32[]{:S(2)}, u32[]{:S(2)}) async-start(bf16[16,288,128]{2,1,0:T(8,128)(2,1)} %bitcast.13), calls=%async_computation.1 | async-start | bytes 2359296 | tf_op jit(solution)/shard_map/all_to_all | solution.py:332
  52.4 0.1 eq.116
  52.5 0.1 copy.56
  52.6 0.1 pad_add_fusion.1
  52.7 20.3 %all-to-all-done.1 = bf16[16,288,128]{2,1,0:T(8,128)(2,1)S(1)} async-done(((bf16[16,288,128]{2,1,0:T(8,128)(2,1)}), bf16[16,288,128]{2,1,0:T(8,128)(2,1)S(1)}, u32[]{:S(2)}, u32[]{:S(2)}) %all-to-all-start.1) | async-done | bytes 1179680 | tf_op jit(solution)/shard_map/all_to_all | solution.py:332
  73.0 0.1 slice.56
  73.1 0.7 fusion
  73.9 0.6 copy.61
  74.6 7.6 %all-to-all-start.2 = ((bf16[32,256,128]{2,1,0:T(8,128)(2,1)}), bf16[32,256,128]{2,1,0:T(8,128)(2,1)S(1)}, u32[]{:S(2)}, u32[]{:S(2)}) async-start(bf16[32,256,128]{2,1,0:T(8,128)(2,1)} %bitcast.65), calls=%async_computation.2 | async-start | bytes 4194304 | tf_op jit(solution)/shard_map/all_to_all | solution.py:378
  82.3 0.7 copy.60
  83.1 0.1 broadcast_in_dim.112
  83.2 0.1 copy.65
  83.3 0.1 reshape.456
  83.4 0.7 iota_reduce_fusion
  84.1 0.8 gather_fusion
  84.9 0.1 gather.14
  85.0 0.1 broadcast_in_dim.109
  85.0 0.1 ge.21
  85.2 32.8 %all-gather.5.cloned.1.call-done.piece_ref = f32[16,128,128]{2,1,0:T(8,128)} async-done(((f32[1,128,128]{2,1,0:T(8,128)}), f32[16,128,128]{2,1,0:T(8,128)}) %all-gather.5.cloned.1.call-update) | async-done | bytes 1048592 | tf_op jit(solution)/shard_map/all_gather | solution.py:343
  118.0 1.2 copy-done.8
  119.2 30.3 %inverse_factor.1.w_ref = f32[512,512]{1,0:T(8,128)S(1)} custom-call(f32[16,128,128]{2,1,0:T(8,128)S(1)} %copy-done.8), custom_call_target="tpu_custom_call" | custom-call | tf_op jit(solution)/shard_map/inverse_factor/pallas_call | solution.py:166
  149.5 1.1 fusion.1
  150.7 9.9 %collective-permute-start = (bf16[6,8,512]{2,1,0:T(8,128)(2,1)S(1)}, bf16[6,8,512]{2,1,0:T(8,128)(2,1)S(1)}, u32[]{:S(2)}, u32[]{:S(2)}) collective-permute-start(bf16[6,8,512]{2,1,0:T(8,128)(2,1)S(1)} %get-tuple-element.30), channel_id=1, source_target_pairs={{0,0},{1,16},{2,32},{3,48},{4,64},{5,80},{6,96},{7,112},{8,8},{9,2... | collective-permute-start | bytes 147464 | tf_op jit(solution)/shard_map/ppermute | solution.py:368
  160.6 0.1 collective-permute-start.1
  160.8 2.3 collective-permute-done
  163.1 7.3 %collective-permute-done.1 = bf16[6,8,512]{2,1,0:T(8,128)(2,1)S(1)} collective-permute-done((bf16[6,8,512]{2,1,0:T(8,128)(2,1)S(1)}, bf16[6,8,512]{2,1,0:T(8,128)(2,1)S(1)}, u32[]{:S(2)}, u32[]{:S(2)}) %collective-permute-start.1) | collective-permute-done | bytes 49184 | tf_op jit(solution)/shard_map/ppermute | solution.py:369
  170.4 0.9 broadcast_in_dim.111
  171.4 5.2 %all-to-all-start.3 = ((bf16[8,96,512]{2,1,0:T(8,128)(2,1)}), bf16[8,96,512]{2,1,0:T(8,128)(2,1)}, u32[]{:S(2)}, u32[]{:S(2)}) async-start(bf16[8,96,512]{2,1,0:T(8,128)(2,1)} %broadcast_in_dim.111), calls=%async_computation.3 | async-start | bytes 1572864 | tf_op jit(solution)/shard_map/all_to_all | solution.py:373
  176.5 0.1 multiply_add_fusion
  176.6 0.1 add.301.index_ref
  176.8 0.6 compare_reduce_fusion.2
  177.4 13.3 %all-to-all-done.3.trail_ref = bf16[8,96,512]{2,1,0:T(8,128)(2,1)} async-done(((bf16[8,96,512]{2,1,0:T(8,128)(2,1)}), bf16[8,96,512]{2,1,0:T(8,128)(2,1)}, u32[]{:S(2)}, u32[]{:S(2)}) %all-to-all-start.3) | async-done | bytes 786464 | tf_op jit(solution)/shard_map/all_to_all | solution.py:373
  190.7 0.7 pack_second.1
  191.4 1.4 copy-done.4
  192.8 3.7 %all-to-all-start.4 = ((bf16[16,512,128]{2,1,0:T(8,128)(2,1)}), bf16[16,512,128]{2,1,0:T(8,128)(2,1)S(1)}, u32[]{:S(2)}, u32[]{:S(2)}) async-start(bf16[16,512,128]{2,1,0:T(8,128)(2,1)} %bitcast.63), calls=%async_computation.4 | async-start | bytes 4194304 | tf_op jit(solution)/shard_map/all_to_all | solution.py:391
  196.5 0.1 reshape.434
  196.6 0.1 copy.54
  196.7 0.1 copy.55
  196.8 0.2 or_reduce_fusion
  197.0 0.6 gather_fusion.1
  197.5 0.1 and_select_fusion
  197.6 0.2 slice_reduce_fusion
  197.8 1.2 compare_reduce_fusion
  199.0 0.1 iota_xor_fusion
  199.1 0.1 compare_select_fusion.3
  199.3 0.1 reshape.453.col_ref
  199.4 0.4 compare_reduce_fusion.1
  199.8 0.1 add_select_fusion
  199.9 0.1 select_n.198.at_ref
  200.1 1.9 copy-done.5
  201.9 9.2 %solve_rows.1 = (f32[1536,512]{1,0:T(8,128)}, bf16[1536,512]{1,0:T(8,128)(2,1)S(1)}, bf16[1536,512]{1,0:T(8,128)(2,1)S(1)}) custom-call(s32[1]{0:T(128)} %bitcast.4.tile_ref, f32[16,384,128]{2,1,0:T(8,128)S(1)} %copy-done.5, f32[512,512]{1,0:T(8,128)S(1)} %inverse_factor.1.w_ref), custom_call_target="tpu_custom_call" | custom-call | tf_op jit(solution)/shard_map/solve_rows/pallas_call | solution.py:214
  211.1 4.9 %trailing_update.1.base_ref = f32[1536,768]{1,0:T(8,128)S(1)} custom-call(bf16[1536,768]{1,0:T(8,128)(2,1)S(1)} %bitcast.61, bf16[1536,512]{1,0:T(8,128)(2,1)S(1)} %get-tuple-element.15.hi_ref, bf16[1536,512]{1,0:T(8,128)(2,1)S(1)} %get-tuple-element.16.lo_ref, bf16[8,96,512]{2,1,0:T(8,128)(2,1)} %all-to-all-done.3.trail_ref), custom_call_target="tpu_custom_call" | custom-call | tf_op jit(solution)/shard_map/trailing_update/pallas_call | solution.py:265
  216.0 2.2 copy-done
  218.2 11.1 %all-to-all-done.4 = bf16[16,512,128]{2,1,0:T(8,128)(2,1)S(1)} async-done(((bf16[16,512,128]{2,1,0:T(8,128)(2,1)}), bf16[16,512,128]{2,1,0:T(8,128)(2,1)S(1)}, u32[]{:S(2)}, u32[]{:S(2)}) %all-to-all-start.4) | async-done | bytes 2097184 | tf_op jit(solution)/shard_map/all_to_all | solution.py:391
  229.4 2.3 copy-done.1
  231.7 5.9 %add_tiles.1 = f32[1536,768]{1,0:T(8,128)} custom-call(s32[96]{0:T(128)S(1)} %select_n.198.at_ref, s32[96]{0:T(128)S(1)} %reshape.453.col_ref, f32[1536,768]{1,0:T(8,128)S(1)} %copy-done.1, bf16[64,128,128]{2,1,0:T(8,128)(2,1)S(1)} %bitcast.64), custom_call_target="tpu_custom_call" | custom-call | tf_op jit(solution)/shard_map/add_tiles/pallas_call | solution.py:295
  (50 shorter events, 0.5 us)
Async XLA Ops:
  7.3 1.7 copy-start.2
  8.9 1.6 copy-start.6
  10.5 0.7 copy-start.9
  12.5 32.9 %copy-start.7 = (bf16[64,128,128]{2,1,0:T(8,128)(2,1)}, bf16[64,128,128]{2,1,0:T(8,128)(2,1)S(1)}, u32[]{:S(2)}) copy-start(bf16[64,128,128]{2,1,0:T(8,128)(2,1)S(1)} %get-tuple-element.17) | copy-start | bytes 6291460
  44.1 8.3 %copy-start.10 = (s32[2,2,64]{2,1,0:T(2,128)S(1)}, s32[2,2,64]{2,1,0:T(2,128)}, u32[]{:S(2)}) copy-start(s32[2,2,64]{2,1,0:T(2,128)} %param.5) | copy-start | bytes 3076
  45.3 27.7 %all-to-all-start.1 = ((bf16[16,288,128]{2,1,0:T(8,128)(2,1)}), bf16[16,288,128]{2,1,0:T(8,128)(2,1)S(1)}, u32[]{:S(2)}, u32[]{:S(2)}) async-start(bf16[16,288,128]{2,1,0:T(8,128)(2,1)} %bitcast.13), calls=%async_computation.1 | async-start | bytes 2359296 | tf_op jit(solution)/shard_map/all_to_all | solution.py:332
  52.4 65.6 %all-gather.5.cloned.1.call-start = ((), (), s32[]{:S(2)}) async-start(), calls=%async_computation.6 | async-start | bytes 1114112 | tf_op jit(solution)/shard_map/all_gather | solution.py:343
  74.6 95.8 %all-to-all-start.2 = ((bf16[32,256,128]{2,1,0:T(8,128)(2,1)}), bf16[32,256,128]{2,1,0:T(8,128)(2,1)S(1)}, u32[]{:S(2)}, u32[]{:S(2)}) async-start(bf16[32,256,128]{2,1,0:T(8,128)(2,1)} %bitcast.65), calls=%async_computation.2 | async-start | bytes 4194304 | tf_op jit(solution)/shard_map/all_to_all | solution.py:378
  82.2 117.8 %all-gather.3.cloned.1.call-start = ((), (), s32[]{:S(2)}) async-start(), calls=%async_computation.5 | async-start | bytes 3342336 | tf_op jit(solution)/shard_map/all_gather | solution.py:344
  118.0 1.2 copy-start.8
  150.7 12.4 %collective-permute-start = (bf16[6,8,512]{2,1,0:T(8,128)(2,1)S(1)}, bf16[6,8,512]{2,1,0:T(8,128)(2,1)S(1)}, u32[]{:S(2)}, u32[]{:S(2)}) collective-permute-start(bf16[6,8,512]{2,1,0:T(8,128)(2,1)S(1)} %get-tuple-element.30), channel_id=1, source_target_pairs={{0,0},{1,16},{2,32},{3,48},{4,64},{5,80},{6,96},{7,112},{8,8},{9,2... | collective-permute-start | bytes 147464 | tf_op jit(solution)/shard_map/ppermute | solution.py:368
  160.6 9.7 %collective-permute-start.1 = (bf16[6,8,512]{2,1,0:T(8,128)(2,1)S(1)}, bf16[6,8,512]{2,1,0:T(8,128)(2,1)S(1)}, u32[]{:S(2)}, u32[]{:S(2)}) collective-permute-start(bf16[6,8,512]{2,1,0:T(8,128)(2,1)S(1)} %get-tuple-element.31), channel_id=1, source_target_pairs={{0,8},{1,24},{2,40},{3,56},{4,72},{5,88},{6,104},{7,120},{8,0},{9,... | collective-permute-start | bytes 147464 | tf_op jit(solution)/shard_map/ppermute | solution.py:369
  171.4 19.3 %all-to-all-start.3 = ((bf16[8,96,512]{2,1,0:T(8,128)(2,1)}), bf16[8,96,512]{2,1,0:T(8,128)(2,1)}, u32[]{:S(2)}, u32[]{:S(2)}) async-start(bf16[8,96,512]{2,1,0:T(8,128)(2,1)} %broadcast_in_dim.111), calls=%async_computation.3 | async-start | bytes 1572864 | tf_op jit(solution)/shard_map/all_to_all | solution.py:373
  191.4 1.4 copy-start.4
  192.8 36.6 %all-to-all-start.4 = ((bf16[16,512,128]{2,1,0:T(8,128)(2,1)}), bf16[16,512,128]{2,1,0:T(8,128)(2,1)S(1)}, u32[]{:S(2)}, u32[]{:S(2)}) async-start(bf16[16,512,128]{2,1,0:T(8,128)(2,1)} %bitcast.63), calls=%async_computation.4 | async-start | bytes 4194304 | tf_op jit(solution)/shard_map/all_to_all | solution.py:391
  200.0 1.9 copy-start.5
  201.9 9.2 %copy-start.3 = (bf16[1,1536,768]{2,1,0:T(8,128)(2,1)S(1)}, bf16[1,1536,768]{2,1,0:T(8,128)(2,1)}, u32[]{:S(2)}) copy-start(bf16[1,1536,768]{2,1,0:T(8,128)(2,1)} %param.3) | copy-start | bytes 7077892
  216.0 2.2 copy-start
  229.4 2.3 copy-start.1
Sparse Core Ops, SparseCore 0:
  74.7 43.2 all-gather.4
  120.4 40.6 all-gather.2

commit v3 on v2

--- a/solution.py
+++ b/solution.py
@@ -20,10 +20,16 @@
 BF16 = jnp.bfloat16
 
 
-def pack_first(place, maps, child, front):
-    def body(place_ref, maps_ref, child_ref, front_ref, panel_ref, tiles_ref):
-        child_no, quarter = place_ref[0], place_ref[1]
-        targets = [maps_ref[child_no, 16 * quarter + b] for b in range(16)]
+def pack_panel(place, maps, child, front):
+    def locate(s, place_ref, maps_ref):
+        found = jnp.int32(-1)
+        for b in range(16):
+            target = maps_ref[place_ref[0], 16 * place_ref[1] + b]
+            found = jnp.where(target == s, b, found)
+        return found
+
+    def body(place_ref, maps_ref, *refs):
+        strips, front_ref, panel_ref = refs[:4], refs[4], refs[5]
 
         def spread(block, at, count):
             for c in range(16):
@@ -34,15 +40,35 @@
                     ).astype(BF16)
 
         for s in range(4):
-            found = jnp.int32(-1)
-            for b in range(16):
-                found = jnp.where(targets[b] == s, b, found)
-            start = pl.multiple_of(jnp.maximum(found, 0) * TILE, TILE)
-            strip = child_ref[:, pl.ds(start, TILE)].astype(F32)
-            spread(jnp.where(found >= 0, strip, 0.0), 32 * s, 4)
+            strip = strips[s][...].astype(F32)
+            spread(jnp.where(locate(s, place_ref, maps_ref) >= 0, strip, 0.0), 32 * s, 4)
         spread(front_ref[...].astype(F32), 128, 12)
+
+    def strip_spec(s):
+        return pl.BlockSpec(
+            (4 * TILE, TILE), lambda i, p, m: (0, jnp.maximum(locate(s, p, m), 0))
+        )
+
+    return pl.pallas_call(
+        body,
+        grid_spec=pltpu.PrefetchScalarGridSpec(
+            num_scalar_prefetch=2,
+            grid=(1,),
+            in_specs=[strip_spec(s) for s in range(4)]
+            + [pl.BlockSpec((12 * TILE, TILE), lambda i, p, m: (0, 0))],
+            out_specs=pl.BlockSpec((16, 224, TILE), lambda i, p, m: (0, 0, 0)),
+        ),
+        out_shape=jax.ShapeDtypeStruct((16, 224, TILE), BF16),
+        compiler_params=pltpu.CompilerParams(vmem_limit_bytes=56 << 20),
+        name="pack_panel",
+    )(place, maps, child, child, child, child, front)
+
+
+def pack_first(place, maps, child):
+    def body(place_ref, maps_ref, child_ref, tiles_ref):
+        child_no, quarter = place_ref[0], place_ref[1]
         for b in range(16):
-            col = targets[b] % 16
+            col = maps_ref[child_no, 16 * quarter + b] % 16
             for a in range(4):
                 to = ((a // 2) ^ (quarter % 2)) * 32 + col * 2 + a % 2
                 tile = child_ref[a * TILE : (a + 1) * TILE, b * TILE : (b + 1) * TILE]
@@ -52,23 +78,13 @@
     return pl.pallas_call(
         body,
         grid=(1,),
-        out_shape=[
-            jax.ShapeDtypeStruct((16, 224, TILE), BF16),
-            jax.ShapeDtypeStruct((64, TILE, TILE), BF16),
-        ],
-        in_specs=[
-            smem,
-            smem,
-            pl.BlockSpec(child.shape, lambda i: (0, 0)),
-            pl.BlockSpec((12 * TILE, TILE), lambda i: (0, 0)),
-        ],
-        out_specs=[
-            pl.BlockSpec((16, 224, TILE), lambda i: (0, 0, 0)),
-            pl.BlockSpec((64, TILE, TILE), lambda i: (0, 0, 0)),
-        ],
-        compiler_params=pltpu.CompilerParams(vmem_limit_bytes=32 << 20),
+        out_shape=jax.ShapeDtypeStruct((64, TILE, TILE), BF16),
+        in_specs=[smem, smem, pl.BlockSpec(child.shape, lambda i: (0, 0))],
+        out_specs=pl.BlockSpec((64, TILE, TILE), lambda i: (0, 0, 0)),
+        compiler_params=pltpu.CompilerParams(vmem_limit_bytes=14 << 20),
+        cost_estimate=pl.CostEstimate(flops=0, bytes_accessed=4 << 20, transcendentals=0),
         name="pack_first",
-    )(place, maps, child, front)
+    )(place, maps, child)
 
 
 def pack_second(index, tiles):
@@ -84,7 +100,7 @@
             pl.BlockSpec(memory_space=pltpu.VMEM),
         ],
         out_specs=pl.BlockSpec(memory_space=pltpu.VMEM),
-        compiler_params=pltpu.CompilerParams(vmem_limit_bytes=16 << 20),
+        compiler_params=pltpu.CompilerParams(vmem_limit_bytes=10 << 20),
         name="pack_second",
     )(index, tiles)
 
@@ -101,67 +117,75 @@
 
 
 def inverse_factor(gathered):
+    group = 16
+
     def body(piece_ref, w_ref, big, small):
-        lane = lax.broadcasted_iota(jnp.int32, (TILE, 2 * KDIM), 1)
-        sub8 = lax.broadcasted_iota(jnp.int32, (8, 2 * TILE), 0)
+        lane = lax.broadcasted_iota(jnp.int32, (group, TILE), 1)
+        sub = lax.broadcasted_iota(jnp.int32, (group, TILE), 0)
+        lane_all = lax.broadcasted_iota(jnp.int32, (TILE, TILE), 1)
+        row_all = lax.broadcasted_iota(jnp.int32, (TILE, TILE), 0)
         for s in range(4):
             for piece in range(16):
                 at = s * TILE + piece * 8
                 for t in range(4):
                     row = (s * 4 + t) * 8
                     big[at : at + 8, t * TILE : (t + 1) * TILE] = piece_ref[piece, row : row + 8, :]
-        row_no = lax.broadcasted_iota(jnp.int32, (KDIM, KDIM), 0)
-        col_no = lax.broadcasted_iota(jnp.int32, (KDIM, KDIM), 1)
-        big[:, KDIM:] = (row_no == col_no).astype(F32)
-        eye = (
-            lax.broadcasted_iota(jnp.int32, (TILE, TILE), 0)
-            == lax.broadcasted_iota(jnp.int32, (TILE, TILE), 1)
-        ).astype(F32)
-
-        def block(j, carry):
-            start = pl.multiple_of(j * TILE, TILE)
-            rows = pl.ds(start, TILE)
-            small[:, :TILE] = big[rows, pl.ds(start, TILE)]
-            small[:, TILE:] = eye
-            for b in range(TILE // 8):
-                lo = 8 * b
-                panel = small[lo : lo + 8, :]
+
+        for j in range(4):
+            start = j * TILE
+            stop = start + TILE
+            small[...] = big[start:stop, start:stop]
+            for b in range(TILE // group):
+                lo = group * b
+                panel = small[lo : lo + group, :]
+                unit = jnp.where(lane == sub + lo, 1.0, 0.0)
                 cols = [
-                    jnp.broadcast_to(panel[:, lo + m : lo + m + 1], (8, TILE)) for m in range(8)
+                    jnp.broadcast_to(panel[:, lo + m : lo + m + 1], (group, TILE))
+                    for m in range(group)
                 ]
-                for m in range(8):
-                    pivot = jnp.broadcast_to(cols[m][m : m + 1], (8, TILE))
-                    inv = lax.rsqrt(pivot)
-                    inv = inv * (1.5 - 0.5 * pivot * inv * inv)
+                for m in range(group):
+                    inv = lax.rsqrt(jnp.broadcast_to(cols[m][m : m + 1], (group, TILE)))
                     low = cols[m] * inv
-                    for n in range(m + 1, 8):
+                    for n in range(m + 1, group):
                         cols[n] = cols[n] - low * (
-                            jnp.broadcast_to(cols[n][m : m + 1], (8, TILE)) * inv
+                            jnp.broadcast_to(cols[n][m : m + 1], (group, TILE)) * inv
                         )
-                    inv2 = jnp.concatenate([inv, inv], axis=1)
-                    low2 = jnp.concatenate([low, low], axis=1)
-                    scaled = jnp.broadcast_to(panel[m : m + 1], (8, 2 * TILE)) * inv2
-                    panel = jnp.where(
-                        sub8 > m, panel - low2 * scaled, jnp.where(sub8 == m, scaled, panel)
+                    low = jnp.where(sub > m, low, 0.0)
+                    keep = jnp.where(sub == m, inv, 1.0)
+                    panel = panel * keep - low * (
+                        jnp.broadcast_to(panel[m : m + 1], (group, TILE)) * inv
                     )
-                small[lo : lo + 8, :] = panel
-                if b < TILE // 8 - 1:
-                    hi = panel.astype(BF16).astype(F32)
-                    rest = panel - hi
-                    left = jnp.concatenate([hi, hi, rest], axis=0)[:, :TILE].astype(BF16)
-                    right = jnp.concatenate([hi, rest, hi], axis=0).astype(BF16)
+                    unit = unit * keep - low * (
+                        jnp.broadcast_to(unit[m : m + 1], (group, TILE)) * inv
+                    )
+                here = (lane >= lo) & (lane < lo + group)
+                final = jnp.where(here, unit, panel)
+                small[lo : lo + group, :] = final
+                if lo + group < TILE:
+                    p_hi = panel.astype(BF16).astype(F32)
+                    f_hi = final.astype(BF16).astype(F32)
+                    left = jnp.concatenate([p_hi, p_hi, panel - p_hi], axis=0).astype(BF16)
+                    right = jnp.concatenate([f_hi, final - f_hi, f_hi], axis=0).astype(BF16)
                     change = lax.dot_general(
                         left, right, (((0,), (0,)), ((), ())), preferred_element_type=F32
                     )
-                    small[lo + 8 :, :] = small[lo + 8 :, :] - change[lo + 8 :, :]
-            upper = split_dot(small[:, TILE:], big[rows, :], ((1,), (0,)))
-            big[rows, :] = upper
-            below = jnp.where(lane >= start + TILE, upper, 0.0)[:, :KDIM]
-            big[...] = big[...] - split_dot(below, upper, ((0,), (0,)))
-            return carry
-
-        lax.fori_loop(0, 4, block, 0)
-        w_ref[...] = jnp.where(row_no >= col_no, big[:, KDIM:], 0.0)
+                    rest = small[lo + group :, :]
+                    in_block = lane_all[lo + group :, :]
+                    in_block = (in_block >= lo) & (in_block < lo + group)
+                    small[lo + group :, :] = jnp.where(in_block, 0.0, rest) - change[lo + group :, :]
+            diag = jnp.where(row_all >= lane_all, small[...], 0.0)
+            if j > 0:
+                left_part = split_dot(diag, big[start:stop, :start], ((1,), (0,)))
+                big[start:stop, :start] = left_part
+            if j < 3:
+                upper = split_dot(diag, big[start:stop, stop:], ((1,), (0,)))
+                if j > 0:
+                    big[stop:, :start] -= split_dot(upper, left_part, ((0,), (0,)))
+                big[stop:, start:stop] = -split_dot(upper, diag, ((0,), (0,)))
+                big[stop:, stop:] -= split_dot(upper, upper, ((0,), (0,)))
+                big[start:stop, stop:] = jnp.zeros((TILE, KDIM - stop), F32)
+            big[start:stop, start:stop] = diag
+        w_ref[...] = big[...]
 
     return pl.pallas_call(
         body,
@@ -170,10 +194,10 @@
         in_specs=[pl.BlockSpec((16, TILE, TILE), lambda i: (0, 0, 0))],
         out_specs=pl.BlockSpec((KDIM, KDIM), lambda i: (0, 0)),
         scratch_shapes=[
-            pltpu.VMEM((KDIM, 2 * KDIM), F32),
-            pltpu.VMEM((TILE, 2 * TILE), F32),
+            pltpu.VMEM((KDIM, KDIM), F32),
+            pltpu.VMEM((TILE, TILE), F32),
         ],
-        compiler_params=pltpu.CompilerParams(vmem_limit_bytes=24 << 20),
+        compiler_params=pltpu.CompilerParams(vmem_limit_bytes=16 << 20),
         name="inverse_factor",
     )(gathered)
 
@@ -232,7 +256,7 @@
             jax.ShapeDtypeStruct((12 * TILE, KDIM), BF16),
             jax.ShapeDtypeStruct((12 * TILE, KDIM), BF16),
         ],
-        compiler_params=pltpu.CompilerParams(vmem_limit_bytes=24 << 20),
+        compiler_params=pltpu.CompilerParams(vmem_limit_bytes=10 << 20),
         name="solve_rows",
     )(first_tile, gathered, inverse)
 
@@ -274,7 +298,7 @@
         out_specs=pl.BlockSpec((2 * TILE, width), lambda n: (n, 0)),
         scratch_shapes=[pltpu.VMEM((6 * TILE, KDIM), BF16)],
         out_shape=jax.ShapeDtypeStruct(front.shape, F32),
-        compiler_params=pltpu.CompilerParams(vmem_limit_bytes=24 << 20),
+        compiler_params=pltpu.CompilerParams(vmem_limit_bytes=10 << 20),
         name="trailing_update",
     )(front, rows_hi, rows_lo, trail)
 
@@ -304,7 +328,7 @@
             out_specs=pl.BlockSpec((TILE, width), lambda lt, a, b: (lt, 0)),
         ),
         out_shape=jax.ShapeDtypeStruct(base.shape, F32),
-        compiler_params=pltpu.CompilerParams(vmem_limit_bytes=24 << 20),
+        compiler_params=pltpu.CompilerParams(vmem_limit_bytes=10 << 20),
         name="add_tiles",
     )(tile_at, col_at, base, tiles)
 
@@ -320,7 +344,8 @@
     front = front_orig[0]
 
     place = jnp.stack([child_no, quarter]).astype(jnp.int32)
-    message, first_tiles = pack_first(place, maps, child_update, front)
+    message = pack_panel(place, maps, child_update, front)
+    first_tiles = pack_first(place, maps, child_update)
     got = lax.all_to_all(message, COL, split_axis=0, concat_axis=0, tiled=True)
     child_piece = got[:, :128].reshape(4, 4, 128, TILE).astype(F32).sum(axis=1).astype(BF16)
     front_piece = got[:4, 128:].reshape(4, 12, PIECE, TILE)

time: 245 us -> 228 us (0.931)
  Pallas kernels: 52.2 us -> 41.1 us
  waiting for transfers between devices: 87.2 us -> 82.1 us
  local copies, waits for them, and re-layouts: 19.5 us -> 17 us
    pallas_call x1, Pallas kernels: 30.3 us -> 16.3 us  [inverse_factor(): pl.pallas_call(body, grid=(1,), out_shape=jax.ShapeDtypeStruct((KDIM, KDI...]
    all_gather x1, waiting for transfers between devices: 32.8 us -> 27.3 us  [per_device(): diag_all = lax.all_gather(chunk[12:].reshape(128, TILE), COL, axis=0)]
    pallas_call x1 -> x2, Pallas kernels: 1.24 us -> 4.08 us  [the longest x1 3.11 us: pack_panel(): pl.pallas_call(body, grid_spec=pltpu.PrefetchScalarGridSpec(num_scalar_pr...]
    unnamed x23 -> x25, local copies, waits for them, and re-layouts: 12.9 us -> 10.3 us
  transfers between devices with their start and end apart: 8 -> 8, of which waited for: 6 -> 6; matrix products, arithmetic and copies ran while one was open for 4% -> 4% of each run, Pallas kernels for 18% -> 14%
where the time goes in v3:
time: 228 us; the launch traced here: 227 us
  waiting for transfers between devices  82.1 us (36%)
  Pallas kernels  41.1 us (18%)
  starting transfers between devices  33.9 us (15%)
  blocking collectives  31.7 us (14%)
  local copies, waits for them, and re-layouts  17 us (7%)
  between operations  14.5 us (6%)
  other arithmetic  4.48 us (2%)
    all_to_all x1, blocking collectives, per_device(): got = lax.all_to_all(message, COL, split_axis=0, concat_axis=0, tiled=True)  31.7 us
    all_to_all x2, waiting for transfers between devices, per_device(): lax.all_to_all(message, ('front',) + ROW, split_axis=0, concat_axis=0, ti...  31.5 us
    all_gather x1, waiting for transfers between devices, per_device(): diag_all = lax.all_gather(chunk[12:].reshape(128, TILE), COL, axis=0)  27.3 us
    pallas_call x1, Pallas kernels, inverse_factor(): pl.pallas_call(body, grid=(1,), out_shape=jax.ShapeDtypeStruct((KDIM, KDI...  16.3 us
    all_to_all x1, waiting for transfers between devices, per_device(): lax.all_to_all(jnp.broadcast_to(piece, (8, 96, KDIM)), ROW, split_axis=0,...  14.1 us
    all_to_all x2, starting transfers between devices, per_device(): lax.all_to_all(message, ('front',) + ROW, split_axis=0, concat_axis=0, ti...  11 us
    unnamed x25, local copies, waits for them, and re-layouts  10.3 us
    pallas_call x1, Pallas kernels, solve_rows(): pl.pallas_call(body, grid_spec=pltpu.PrefetchScalarGridSpec(num_scalar_pr...  9.19 us
  transfers between devices with their start and end apart: 8, of which 6 were waited for; matrix products, arithmetic and copies ran while one was open for 4% of the time, Pallas kernels for 14%

profile of v3, /device:TPU:32, one launch (start us, length us, event | category | flops | bytes accessed | tf_op | source)
XLA Modules:
  0.0 226.7 jit_solution(13431951472840818535)
XLA Ops:
  7.2 0.6 pad_add_fusion.2.place_ref
  7.8 3.1 %pack_panel.1 = bf16[16,224,128]{2,1,0:T(8,128)(2,1)} custom-call(s32[2]{0:T(128)} %pad_add_fusion.2.place_ref, s32[4,64]{1,0:T(4,128)} %bitcast.66, bf16[512,2048]{1,0:T(8,128)(2,1)} %child_ref.1, bf16[512,2048]{1,0:T(8,128)(2,1)} %child_ref.1, bf16[512,2048]{1,0:T(8,128)(2,1)} %child_ref.1, bf16[512,2048]{1,0:T(8,128)(2,1)} %child_ref.1, ...), custom_call_target="tpu_custom_call" | custom-call | tf_op jit(solution)/shard_map/pack_panel/pallas_call | solution.py:52
  10.9 31.7 %all_to_all.25 = bf16[16,224,128]{2,1,0:T(8,128)(2,1)S(1)} all-to-all(bf16[16,224,128]{2,1,0:T(8,128)(2,1)} %pack_panel.1), channel_id=1, replica_groups=mesh['front'=2,'rowh'=4,'xlo'=2,'z'=8,'core'=2] {'z','core'}, dimensions={0} | all-to-all | bytes 1835008 | tf_op jit(solution)/shard_map/all_to_all | solution.py:349
  42.6 0.1 bitcast_reduce_fusion
  42.8 1.2 broadcast_in_dim.108
  43.9 7.0 %all-to-all-start.1 = ((bf16[16,288,128]{2,1,0:T(8,128)(2,1)}), bf16[16,288,128]{2,1,0:T(8,128)(2,1)S(1)}, u32[]{:S(2)}, u32[]{:S(2)}) async-start(bf16[16,288,128]{2,1,0:T(8,128)(2,1)} %bitcast.13), calls=%async_computation.1 | async-start | bytes 2359296 | tf_op jit(solution)/shard_map/all_to_all | solution.py:357
  51.1 0.1 eq.116
  51.1 0.1 copy.56
  51.2 0.1 pad_add_fusion.1
  51.3 20.3 %all-to-all-done.1 = bf16[16,288,128]{2,1,0:T(8,128)(2,1)S(1)} async-done(((bf16[16,288,128]{2,1,0:T(8,128)(2,1)}), bf16[16,288,128]{2,1,0:T(8,128)(2,1)S(1)}, u32[]{:S(2)}, u32[]{:S(2)}) %all-to-all-start.1) | async-done | bytes 1179680 | tf_op jit(solution)/shard_map/all_to_all | solution.py:357
  71.6 0.1 slice.56
  71.8 0.7 fusion
  72.5 0.7 copy.61
  73.3 1.0 pack_first.1
  74.3 1.3 copy-done.4
  75.6 7.7 %all-to-all-start.2 = ((bf16[32,256,128]{2,1,0:T(8,128)(2,1)}), bf16[32,256,128]{2,1,0:T(8,128)(2,1)S(1)}, u32[]{:S(2)}, u32[]{:S(2)}) async-start(bf16[32,256,128]{2,1,0:T(8,128)(2,1)} %bitcast.63), calls=%async_computation.2 | async-start | bytes 4194304 | tf_op jit(solution)/shard_map/all_to_all | solution.py:403
  83.3 0.2 all-gather.3.cloned.1.call-start
  83.6 0.7 copy.60
  84.4 0.1 broadcast_in_dim.112
  84.5 0.1 copy.65
  84.6 0.1 reshape.456
  84.7 0.7 iota_reduce_fusion
  85.5 0.8 gather_fusion
  86.2 0.1 gather.14
  86.3 0.1 broadcast_in_dim.109
  86.4 0.1 ge.21
  86.5 27.3 %all-gather.5.cloned.1.call-done.piece_ref = f32[16,128,128]{2,1,0:T(8,128)} async-done(((f32[1,128,128]{2,1,0:T(8,128)}), f32[16,128,128]{2,1,0:T(8,128)}) %all-gather.5.cloned.1.call-update) | async-done | bytes 1048592 | tf_op jit(solution)/shard_map/all_gather | solution.py:368
  113.8 1.2 copy-done.7
  115.1 16.3 %inverse_factor.1.w_ref = f32[512,512]{1,0:T(8,128)S(1)} custom-call(f32[16,128,128]{2,1,0:T(8,128)S(1)} %copy-done.7), custom_call_target="tpu_custom_call" | custom-call | tf_op jit(solution)/shard_map/inverse_factor/pallas_call | solution.py:190
  131.4 1.1 fusion.1
  132.6 7.9 %collective-permute-start = (bf16[6,8,512]{2,1,0:T(8,128)(2,1)S(1)}, bf16[6,8,512]{2,1,0:T(8,128)(2,1)S(1)}, u32[]{:S(2)}, u32[]{:S(2)}) collective-permute-start(bf16[6,8,512]{2,1,0:T(8,128)(2,1)S(1)} %get-tuple-element.26), channel_id=1, source_target_pairs={{0,0},{1,16},{2,32},{3,48},{4,64},{5,80},{6,96},{7,112},{8,8},{9,2... | collective-permute-start | bytes 147464 | tf_op jit(solution)/shard_map/ppermute | solution.py:393
  140.5 1.7 collective-permute-start.1
  142.2 1.2 collective-permute-done
  143.4 8.0 %collective-permute-done.1 = bf16[6,8,512]{2,1,0:T(8,128)(2,1)S(1)} collective-permute-done((bf16[6,8,512]{2,1,0:T(8,128)(2,1)S(1)}, bf16[6,8,512]{2,1,0:T(8,128)(2,1)S(1)}, u32[]{:S(2)}, u32[]{:S(2)}) %collective-permute-start.1) | collective-permute-done | bytes 49184 | tf_op jit(solution)/shard_map/ppermute | solution.py:394
  151.4 0.9 broadcast_in_dim.111
  152.4 5.3 %all-to-all-start.3 = ((bf16[8,96,512]{2,1,0:T(8,128)(2,1)}), bf16[8,96,512]{2,1,0:T(8,128)(2,1)}, u32[]{:S(2)}, u32[]{:S(2)}) async-start(bf16[8,96,512]{2,1,0:T(8,128)(2,1)} %broadcast_in_dim.111), calls=%async_computation.3 | async-start | bytes 1572864 | tf_op jit(solution)/shard_map/all_to_all | solution.py:398
  157.7 0.1 multiply_add_fusion
  157.8 0.1 add.301.index_ref
  157.9 0.6 compare_reduce_fusion.2
  158.6 14.1 %all-to-all-done.3.trail_ref = bf16[8,96,512]{2,1,0:T(8,128)(2,1)} async-done(((bf16[8,96,512]{2,1,0:T(8,128)(2,1)}), bf16[8,96,512]{2,1,0:T(8,128)(2,1)}, u32[]{:S(2)}, u32[]{:S(2)}) %all-to-all-start.3) | async-done | bytes 786464 | tf_op jit(solution)/shard_map/all_to_all | solution.py:398
  172.7 0.7 pack_second.1
  173.4 1.4 copy-done.5
  174.7 3.9 %all-to-all-start.4 = ((bf16[16,512,128]{2,1,0:T(8,128)(2,1)}), bf16[16,512,128]{2,1,0:T(8,128)(2,1)S(1)}, u32[]{:S(2)}, u32[]{:S(2)}) async-start(bf16[16,512,128]{2,1,0:T(8,128)(2,1)} %bitcast.64), calls=%async_computation.4 | async-start | bytes 4194304 | tf_op jit(solution)/shard_map/all_to_all | solution.py:416
  178.7 0.1 reshape.434
  178.8 0.1 copy.54
  178.9 0.1 copy.55
  178.9 0.2 or_reduce_fusion
  179.1 0.6 gather_fusion.1
  179.7 0.1 and_select_fusion
  179.8 0.2 slice_reduce_fusion
  180.0 1.2 compare_reduce_fusion
  181.2 0.1 iota_xor_fusion
  181.3 0.1 compare_select_fusion.3
  181.4 0.1 reshape.453.col_ref
  181.6 0.4 compare_reduce_fusion.1
  181.9 0.1 add_select_fusion
  182.1 0.1 select_n.198.at_ref
  182.2 1.9 copy-done.6
  184.1 9.2 %solve_rows.1 = (f32[1536,512]{1,0:T(8,128)}, bf16[1536,512]{1,0:T(8,128)(2,1)S(1)}, bf16[1536,512]{1,0:T(8,128)(2,1)S(1)}) custom-call(s32[1]{0:T(128)} %bitcast.4.tile_ref, f32[16,384,128]{2,1,0:T(8,128)S(1)} %copy-done.6, f32[512,512]{1,0:T(8,128)S(1)} %inverse_factor.1.w_ref), custom_call_target="tpu_custom_call" | custom-call | tf_op jit(solution)/shard_map/solve_rows/pallas_call | solution.py:238
  193.3 4.9 %trailing_update.1.base_ref = f32[1536,768]{1,0:T(8,128)S(1)} custom-call(bf16[1536,768]{1,0:T(8,128)(2,1)S(1)} %bitcast.61, bf16[1536,512]{1,0:T(8,128)(2,1)S(1)} %get-tuple-element.12.hi_ref, bf16[1536,512]{1,0:T(8,128)(2,1)S(1)} %get-tuple-element.13.lo_ref, bf16[8,96,512]{2,1,0:T(8,128)(2,1)} %all-to-all-done.3.trail_ref), custom_call_target="tpu_custom_call" | custom-call | tf_op jit(solution)/shard_map/trailing_update/pallas_call | solution.py:289
  198.2 2.2 copy-done.1
  200.4 11.2 %all-to-all-done.4 = bf16[16,512,128]{2,1,0:T(8,128)(2,1)S(1)} async-done(((bf16[16,512,128]{2,1,0:T(8,128)(2,1)}), bf16[16,512,128]{2,1,0:T(8,128)(2,1)S(1)}, u32[]{:S(2)}, u32[]{:S(2)}) %all-to-all-start.4) | async-done | bytes 2097184 | tf_op jit(solution)/shard_map/all_to_all | solution.py:416
  211.6 2.3 %copy-done.2 = f32[1536,768]{1,0:T(8,128)S(1)} copy-done((f32[1536,768]{1,0:T(8,128)S(1)}, f32[1536,768]{1,0:T(8,128)}, u32[]{:S(2)}) %copy-start.2) | copy-done | bytes 4718616
  213.9 5.9 %add_tiles.1 = f32[1536,768]{1,0:T(8,128)} custom-call(s32[96]{0:T(128)S(1)} %select_n.198.at_ref, s32[96]{0:T(128)S(1)} %reshape.453.col_ref, f32[1536,768]{1,0:T(8,128)S(1)} %copy-done.2, bf16[64,128,128]{2,1,0:T(8,128)(2,1)S(1)} %bitcast.65), custom_call_target="tpu_custom_call" | custom-call | tf_op jit(solution)/shard_map/add_tiles/pallas_call | solution.py:319
  (53 shorter events, 0.5 us)
Async XLA Ops:
  42.7 8.3 %copy-start.8 = (s32[2,2,64]{2,1,0:T(2,128)S(1)}, s32[2,2,64]{2,1,0:T(2,128)}, u32[]{:S(2)}) copy-start(s32[2,2,64]{2,1,0:T(2,128)} %param.5) | copy-start | bytes 3076
  43.9 27.7 %all-to-all-start.1 = ((bf16[16,288,128]{2,1,0:T(8,128)(2,1)}), bf16[16,288,128]{2,1,0:T(8,128)(2,1)S(1)}, u32[]{:S(2)}, u32[]{:S(2)}) async-start(bf16[16,288,128]{2,1,0:T(8,128)(2,1)} %bitcast.13), calls=%async_computation.1 | async-start | bytes 2359296 | tf_op jit(solution)/shard_map/all_to_all | solution.py:357
  51.0 62.9 %all-gather.5.cloned.1.call-start = ((), (), s32[]{:S(2)}) async-start(), calls=%async_computation.6 | async-start | bytes 1114112 | tf_op jit(solution)/shard_map/all_gather | solution.py:368
  71.6 1.6 copy-start
  71.6 1.6 copy-start.9
  72.5 1.8 copy-start.10
  74.2 1.3 copy-start.4
  75.6 8.0 %copy-start.11 = (f32[16,4,8,128]{3,0,2,1:T(8,128)S(1)}, f32[16,4,8,128]{3,0,2,1:T(8,128)}, u32[]{:S(2)}) copy-start(f32[16,4,8,128]{3,0,2,1:T(8,128)} %copy-done.10) | copy-start | bytes 786436
  75.6 75.8 %all-to-all-start.2 = ((bf16[32,256,128]{2,1,0:T(8,128)(2,1)}), bf16[32,256,128]{2,1,0:T(8,128)(2,1)S(1)}, u32[]{:S(2)}, u32[]{:S(2)}) async-start(bf16[32,256,128]{2,1,0:T(8,128)(2,1)} %bitcast.63), calls=%async_computation.2 | async-start | bytes 4194304 | tf_op jit(solution)/shard_map/all_to_all | solution.py:403
  83.3 98.9 %all-gather.3.cloned.1.call-start = ((), (), s32[]{:S(2)}) async-start(), calls=%async_computation.5 | async-start | bytes 3342336 | tf_op jit(solution)/shard_map/all_gather | solution.py:369
  113.8 1.2 copy-start.7
  132.6 10.8 %collective-permute-start = (bf16[6,8,512]{2,1,0:T(8,128)(2,1)S(1)}, bf16[6,8,512]{2,1,0:T(8,128)(2,1)S(1)}, u32[]{:S(2)}, u32[]{:S(2)}) collective-permute-start(bf16[6,8,512]{2,1,0:T(8,128)(2,1)S(1)} %get-tuple-element.26), channel_id=1, source_target_pairs={{0,0},{1,16},{2,32},{3,48},{4,64},{5,80},{6,96},{7,112},{8,8},{9,2... | collective-permute-start | bytes 147464 | tf_op jit(solution)/shard_map/ppermute | solution.py:393
  140.5 10.9 %collective-permute-start.1 = (bf16[6,8,512]{2,1,0:T(8,128)(2,1)S(1)}, bf16[6,8,512]{2,1,0:T(8,128)(2,1)S(1)}, u32[]{:S(2)}, u32[]{:S(2)}) collective-permute-start(bf16[6,8,512]{2,1,0:T(8,128)(2,1)S(1)} %get-tuple-element.27), channel_id=1, source_target_pairs={{0,8},{1,24},{2,40},{3,56},{4,72},{5,88},{6,104},{7,120},{8,0},{9,... | collective-permute-start | bytes 147464 | tf_op jit(solution)/shard_map/ppermute | solution.py:394
  152.4 20.3 %all-to-all-start.3 = ((bf16[8,96,512]{2,1,0:T(8,128)(2,1)}), bf16[8,96,512]{2,1,0:T(8,128)(2,1)}, u32[]{:S(2)}, u32[]{:S(2)}) async-start(bf16[8,96,512]{2,1,0:T(8,128)(2,1)} %broadcast_in_dim.111), calls=%async_computation.3 | async-start | bytes 1572864 | tf_op jit(solution)/shard_map/all_to_all | solution.py:398
  173.3 1.4 copy-start.5
  174.7 36.9 %all-to-all-start.4 = ((bf16[16,512,128]{2,1,0:T(8,128)(2,1)}), bf16[16,512,128]{2,1,0:T(8,128)(2,1)S(1)}, u32[]{:S(2)}, u32[]{:S(2)}) async-start(bf16[16,512,128]{2,1,0:T(8,128)(2,1)} %bitcast.64), calls=%async_computation.4 | async-start | bytes 4194304 | tf_op jit(solution)/shard_map/all_to_all | solution.py:416
  182.2 1.9 copy-start.6
  184.1 9.2 %copy-start.3 = (bf16[1,1536,768]{2,1,0:T(8,128)(2,1)S(1)}, bf16[1,1536,768]{2,1,0:T(8,128)(2,1)}, u32[]{:S(2)}) copy-start(bf16[1,1536,768]{2,1,0:T(8,128)(2,1)} %param.3) | copy-start | bytes 7077892
  198.2 2.2 copy-start.1
  211.6 2.3 %copy-start.2 = (f32[1536,768]{1,0:T(8,128)S(1)}, f32[1536,768]{1,0:T(8,128)}, u32[]{:S(2)}) copy-start(f32[1536,768]{1,0:T(8,128)} %copy-done.1) | copy-start | bytes 14155780
Sparse Core Ops, SparseCore 0:
  73.4 40.4 all-gather.4
  116.2 47.0 all-gather.2

commit v4 on v3

--- a/solution.py
+++ b/solution.py
@@ -298,37 +298,43 @@
         out_specs=pl.BlockSpec((2 * TILE, width), lambda n: (n, 0)),
         scratch_shapes=[pltpu.VMEM((6 * TILE, KDIM), BF16)],
         out_shape=jax.ShapeDtypeStruct(front.shape, F32),
-        compiler_params=pltpu.CompilerParams(vmem_limit_bytes=10 << 20),
+        compiler_params=pltpu.CompilerParams(vmem_limit_bytes=56 << 20),
         name="trailing_update",
     )(front, rows_hi, rows_lo, trail)
 
 
 def add_tiles(tile_at, col_at, base, tiles):
+    per_step = 3
+
     def body(at_ref, col_ref, base_ref, tiles_ref, out_ref):
-        lt = pl.program_id(0)
         out_ref[...] = base_ref[...]
-        for n in range(8):
-            source = at_ref[lt * 8 + n]
-
-            @pl.when(source >= 0)
-            def _():
-                where_col = pl.multiple_of(col_ref[lt * 8 + n] * TILE, TILE)
-                out_ref[:, pl.ds(where_col, TILE)] += tiles_ref[source].astype(F32)
-
-    width = base.shape[1]
+        for m in range(per_step):
+            for n in range(8):
+                entry = (pl.program_id(0) * per_step + m) * 8 + n
+                source = at_ref[entry]
+
+                @pl.when(source >= 0)
+                def _():
+                    where_col = pl.multiple_of(col_ref[entry] * TILE, TILE)
+                    out_ref[m * TILE : (m + 1) * TILE, pl.ds(where_col, TILE)] += tiles_ref[
+                        source
+                    ].astype(F32)
+
+    block = (per_step * TILE, base.shape[1])
     return pl.pallas_call(
         body,
         grid_spec=pltpu.PrefetchScalarGridSpec(
             num_scalar_prefetch=2,
-            grid=(12,),
+            grid=(12 // per_step,),
             in_specs=[
-                pl.BlockSpec((TILE, width), lambda lt, a, b: (lt, 0)),
-                pl.BlockSpec((64, TILE, TILE), lambda lt, a, b: (0, 0, 0)),
+                pl.BlockSpec(block, lambda step, a, b: (step, 0)),
+                pl.BlockSpec((64, TILE, TILE), lambda step, a, b: (0, 0, 0)),
             ],
-            out_specs=pl.BlockSpec((TILE, width), lambda lt, a, b: (lt, 0)),
+            out_specs=pl.BlockSpec(block, lambda step, a, b: (step, 0)),
         ),
         out_shape=jax.ShapeDtypeStruct(base.shape, F32),
-        compiler_params=pltpu.CompilerParams(vmem_limit_bytes=10 << 20),
+        input_output_aliases={2: 0},
+        compiler_params=pltpu.CompilerParams(vmem_limit_bytes=14 << 20),
         name="add_tiles",
     )(tile_at, col_at, base, tiles)
 

time: 228 us -> 226 us (level)
  waiting for transfers between devices: 82.1 us -> 78.7 us
  Pallas kernels: 41.1 us -> 44.4 us
  local copies, waits for them, and re-layouts: 17 us -> 14.7 us
    all_to_all x2, waiting for transfers between devices: 31.5 us -> 28.3 us  [per_device(): lax.all_to_all(message, ('front',) + ROW, split_axis=0, concat_axis=0, ti...]
    pallas_call x1, Pallas kernels: 4.89 us -> 7.89 us  [trailing_update(): pl.pallas_call(body, grid=(6,), in_specs=[pl.BlockSpec((2 * TILE, width),...]
    unnamed x25 -> x23, local copies, waits for them, and re-layouts: 10.3 us -> 8.11 us
  transfers between devices with their start and end apart: 8 -> 8, of which waited for: 6 -> 6; matrix products, arithmetic and copies ran while one was open for 4% -> 4% of each run, Pallas kernels for 14% -> 16%
where the time goes in v4:
time: 226 us; the launch traced here: 224 us
  waiting for transfers between devices  78.7 us (35%)
  Pallas kernels  44.4 us (20%)
  starting transfers between devices  33.8 us (15%)
  blocking collectives  31.8 us (14%)
  local copies, waits for them, and re-layouts  14.7 us (7%)
  between operations  14.5 us (6%)
  other arithmetic  4.48 us (2%)
    all_to_all x1, blocking collectives, per_device(): got = lax.all_to_all(message, COL, split_axis=0, concat_axis=0, tiled=True)  31.8 us
    all_to_all x2, waiting for transfers between devices, per_device(): lax.all_to_all(message, ('front',) + ROW, split_axis=0, concat_axis=0, ti...  28.3 us
    all_gather x1, waiting for transfers between devices, per_device(): diag_all = lax.all_gather(chunk[12:].reshape(128, TILE), COL, axis=0)  27.3 us
    pallas_call x1, Pallas kernels, inverse_factor(): pl.pallas_call(body, grid=(1,), out_shape=jax.ShapeDtypeStruct((KDIM, KDI...  16.3 us
    all_to_all x1, waiting for transfers between devices, per_device(): lax.all_to_all(jnp.broadcast_to(piece, (8, 96, KDIM)), ROW, split_axis=0,...  13.8 us
    all_to_all x2, starting transfers between devices, per_device(): lax.all_to_all(message, ('front',) + ROW, split_axis=0, concat_axis=0, ti...  11 us
    pallas_call x1, Pallas kernels, solve_rows(): pl.pallas_call(body, grid_spec=pltpu.PrefetchScalarGridSpec(num_scalar_pr...  9.18 us
    unnamed x23, local copies, waits for them, and re-layouts  8.11 us
  transfers between devices with their start and end apart: 8, of which 6 were waited for; matrix products, arithmetic and copies ran while one was open for 4% of the time, Pallas kernels for 16%

profile of v4, /device:TPU:32, one launch (start us, length us, event | category | flops | bytes accessed | tf_op | source)
XLA Modules:
  0.0 224.3 jit_solution(8708502858185797672)
XLA Ops:
  7.2 0.6 pad_add_fusion.2.place_ref
  7.8 3.1 %pack_panel.1 = bf16[16,224,128]{2,1,0:T(8,128)(2,1)} custom-call(s32[2]{0:T(128)} %pad_add_fusion.2.place_ref, s32[4,64]{1,0:T(4,128)} %bitcast.64, bf16[512,2048]{1,0:T(8,128)(2,1)} %child_ref.1, bf16[512,2048]{1,0:T(8,128)(2,1)} %child_ref.1, bf16[512,2048]{1,0:T(8,128)(2,1)} %child_ref.1, bf16[512,2048]{1,0:T(8,128)(2,1)} %child_ref.1, ...), custom_call_target="tpu_custom_call" | custom-call | tf_op jit(solution)/shard_map/pack_panel/pallas_call | solution.py:52
  10.9 31.8 %all_to_all.25 = bf16[16,224,128]{2,1,0:T(8,128)(2,1)S(1)} all-to-all(bf16[16,224,128]{2,1,0:T(8,128)(2,1)} %pack_panel.1), channel_id=1, replica_groups=mesh['front'=2,'rowh'=4,'xlo'=2,'z'=8,'core'=2] {'z','core'}, dimensions={0} | all-to-all | bytes 1835008 | tf_op jit(solution)/shard_map/all_to_all | solution.py:355
  42.7 0.1 bitcast_reduce_fusion
  42.8 1.2 broadcast_in_dim.108
  44.0 7.0 %all-to-all-start.1 = ((bf16[16,288,128]{2,1,0:T(8,128)(2,1)}), bf16[16,288,128]{2,1,0:T(8,128)(2,1)S(1)}, u32[]{:S(2)}, u32[]{:S(2)}) async-start(bf16[16,288,128]{2,1,0:T(8,128)(2,1)} %bitcast.13), calls=%async_computation.1 | async-start | bytes 2359296 | tf_op jit(solution)/shard_map/all_to_all | solution.py:363
  51.1 0.1 eq.116
  51.2 0.1 copy.57
  51.3 0.1 pad_add_fusion.1
  51.4 20.3 %all-to-all-done.1 = bf16[16,288,128]{2,1,0:T(8,128)(2,1)S(1)} async-done(((bf16[16,288,128]{2,1,0:T(8,128)(2,1)}), bf16[16,288,128]{2,1,0:T(8,128)(2,1)S(1)}, u32[]{:S(2)}, u32[]{:S(2)}) %all-to-all-start.1) | async-done | bytes 1179680 | tf_op jit(solution)/shard_map/all_to_all | solution.py:363
  71.7 0.1 slice.56
  71.8 0.7 fusion
  72.6 0.7 copy.62
  73.3 1.0 pack_first.1
  74.3 1.3 copy-done.1
  75.6 7.7 %all-to-all-start.2 = ((bf16[32,256,128]{2,1,0:T(8,128)(2,1)}), bf16[32,256,128]{2,1,0:T(8,128)(2,1)S(1)}, u32[]{:S(2)}, u32[]{:S(2)}) async-start(bf16[32,256,128]{2,1,0:T(8,128)(2,1)} %bitcast.61), calls=%async_computation.2 | async-start | bytes 4194304 | tf_op jit(solution)/shard_map/all_to_all | solution.py:409
  83.4 0.2 all-gather.3.cloned.1.call-start
  83.7 0.7 copy.61
  84.5 0.1 broadcast_in_dim.112
  84.6 0.1 copy.66
  84.7 0.1 reshape.456
  84.8 0.7 iota_reduce_fusion
  85.5 0.8 gather_fusion
  86.3 0.1 gather.14
  86.4 0.1 broadcast_in_dim.109
  86.5 0.1 ge.21
  86.6 27.3 %all-gather.5.cloned.1.call-done.piece_ref = f32[16,128,128]{2,1,0:T(8,128)} async-done(((f32[1,128,128]{2,1,0:T(8,128)}), f32[16,128,128]{2,1,0:T(8,128)}) %all-gather.5.cloned.1.call-update) | async-done | bytes 1048592 | tf_op jit(solution)/shard_map/all_gather | solution.py:374
  113.9 1.2 copy-done.6
  115.1 16.3 %inverse_factor.1.w_ref = f32[512,512]{1,0:T(8,128)S(1)} custom-call(f32[16,128,128]{2,1,0:T(8,128)S(1)} %copy-done.6), custom_call_target="tpu_custom_call" | custom-call | tf_op jit(solution)/shard_map/inverse_factor/pallas_call | solution.py:190
  131.5 1.1 fusion.1
  132.6 7.9 %collective-permute-start = (bf16[6,8,512]{2,1,0:T(8,128)(2,1)S(1)}, bf16[6,8,512]{2,1,0:T(8,128)(2,1)S(1)}, u32[]{:S(2)}, u32[]{:S(2)}) collective-permute-start(bf16[6,8,512]{2,1,0:T(8,128)(2,1)S(1)} %get-tuple-element.26), channel_id=1, source_target_pairs={{0,0},{1,16},{2,32},{3,48},{4,64},{5,80},{6,96},{7,112},{8,8},{9,2... | collective-permute-start | bytes 147464 | tf_op jit(solution)/shard_map/ppermute | solution.py:399
  140.6 1.7 collective-permute-start.1
  142.3 1.2 collective-permute-done
  143.5 8.1 %collective-permute-done.1 = bf16[6,8,512]{2,1,0:T(8,128)(2,1)S(1)} collective-permute-done((bf16[6,8,512]{2,1,0:T(8,128)(2,1)S(1)}, bf16[6,8,512]{2,1,0:T(8,128)(2,1)S(1)}, u32[]{:S(2)}, u32[]{:S(2)}) %collective-permute-start.1) | collective-permute-done | bytes 49184 | tf_op jit(solution)/shard_map/ppermute | solution.py:400
  151.6 0.9 broadcast_in_dim.111
  152.6 5.2 %all-to-all-start.3 = ((bf16[8,96,512]{2,1,0:T(8,128)(2,1)}), bf16[8,96,512]{2,1,0:T(8,128)(2,1)}, u32[]{:S(2)}, u32[]{:S(2)}) async-start(bf16[8,96,512]{2,1,0:T(8,128)(2,1)} %broadcast_in_dim.111), calls=%async_computation.3 | async-start | bytes 1572864 | tf_op jit(solution)/shard_map/all_to_all | solution.py:404
  157.8 0.1 multiply_add_fusion
  157.9 0.1 add.301.index_ref
  158.0 0.6 compare_reduce_fusion.2
  158.6 13.8 %all-to-all-done.3.trail_ref = bf16[8,96,512]{2,1,0:T(8,128)(2,1)} async-done(((bf16[8,96,512]{2,1,0:T(8,128)(2,1)}), bf16[8,96,512]{2,1,0:T(8,128)(2,1)}, u32[]{:S(2)}, u32[]{:S(2)}) %all-to-all-start.3) | async-done | bytes 786464 | tf_op jit(solution)/shard_map/all_to_all | solution.py:404
  172.4 0.7 pack_second.1
  173.1 1.4 copy-done.2
  174.5 3.9 %all-to-all-start.4 = ((bf16[16,512,128]{2,1,0:T(8,128)(2,1)}), bf16[16,512,128]{2,1,0:T(8,128)(2,1)S(1)}, u32[]{:S(2)}, u32[]{:S(2)}) async-start(bf16[16,512,128]{2,1,0:T(8,128)(2,1)} %bitcast.62), calls=%async_computation.4 | async-start | bytes 4194304 | tf_op jit(solution)/shard_map/all_to_all | solution.py:422
  178.5 0.1 reshape.434
  178.6 0.1 copy.55
  178.6 0.1 copy.56
  178.7 0.2 or_reduce_fusion
  178.9 0.6 gather_fusion.1
  179.5 0.1 and_select_fusion
  179.6 0.2 slice_reduce_fusion
  179.8 1.2 compare_reduce_fusion
  181.0 0.1 iota_xor_fusion
  181.1 0.1 compare_select_fusion.3
  181.2 0.1 reshape.453.col_ref
  181.4 0.4 compare_reduce_fusion.1
  181.7 0.1 add_select_fusion
  181.9 0.1 select_n.198.at_ref
  182.0 1.9 copy-done.3
  183.9 9.2 %solve_rows.1 = (f32[1536,512]{1,0:T(8,128)}, bf16[1536,512]{1,0:T(8,128)(2,1)S(1)}, bf16[1536,512]{1,0:T(8,128)(2,1)S(1)}) custom-call(s32[1]{0:T(128)} %bitcast.4.tile_ref, f32[16,384,128]{2,1,0:T(8,128)S(1)} %copy-done.3, f32[512,512]{1,0:T(8,128)S(1)} %inverse_factor.1.w_ref), custom_call_target="tpu_custom_call" | custom-call | tf_op jit(solution)/shard_map/solve_rows/pallas_call | solution.py:238
  193.1 1.2 copy-done.4
  194.2 1.1 copy-done.5
  195.4 7.9 %trailing_update.1.base_ref = f32[1536,768]{1,0:T(8,128)} custom-call(bf16[1536,768]{1,0:T(8,128)(2,1)} %bitcast.70, bf16[1536,512]{1,0:T(8,128)(2,1)} %copy-done.4, bf16[1536,512]{1,0:T(8,128)(2,1)} %copy-done.5, bf16[8,96,512]{2,1,0:T(8,128)(2,1)} %all-to-all-done.3.trail_ref), custom_call_target="tpu_custom_call" | custom-call | tf_op jit(solution)/shard_map/trailing_update/pallas_call | solution.py:289
  203.3 8.0 %all-to-all-done.4 = bf16[16,512,128]{2,1,0:T(8,128)(2,1)S(1)} async-done(((bf16[16,512,128]{2,1,0:T(8,128)(2,1)}), bf16[16,512,128]{2,1,0:T(8,128)(2,1)S(1)}, u32[]{:S(2)}, u32[]{:S(2)}) %all-to-all-start.4) | async-done | bytes 2097184 | tf_op jit(solution)/shard_map/all_to_all | solution.py:422
  211.3 6.2 %add_tiles.1 = f32[1536,768]{1,0:T(8,128)} custom-call(s32[96]{0:T(128)S(1)} %select_n.198.at_ref, s32[96]{0:T(128)S(1)} %reshape.453.col_ref, f32[1536,768]{1,0:T(8,128)} %trailing_update.1.base_ref, bf16[64,128,128]{2,1,0:T(8,128)(2,1)S(1)} %bitcast.63), custom_call_target="tpu_custom_call", output_to_operand_aliasing={{}: (2, {})} | custom-call | tf_op jit(solution)/shard_map/add_tiles/pallas_call | solution.py:324
  (51 shorter events, 0.5 us)
Async XLA Ops:
  42.8 8.3 %copy-start.7 = (s32[2,2,64]{2,1,0:T(2,128)S(1)}, s32[2,2,64]{2,1,0:T(2,128)}, u32[]{:S(2)}) copy-start(s32[2,2,64]{2,1,0:T(2,128)} %param.5) | copy-start | bytes 3076
  44.0 27.7 %all-to-all-start.1 = ((bf16[16,288,128]{2,1,0:T(8,128)(2,1)}), bf16[16,288,128]{2,1,0:T(8,128)(2,1)S(1)}, u32[]{:S(2)}, u32[]{:S(2)}) async-start(bf16[16,288,128]{2,1,0:T(8,128)(2,1)} %bitcast.13), calls=%async_computation.1 | async-start | bytes 2359296 | tf_op jit(solution)/shard_map/all_to_all | solution.py:363
  51.0 62.9 %all-gather.5.cloned.1.call-start = ((), (), s32[]{:S(2)}) async-start(), calls=%async_computation.6 | async-start | bytes 1114112 | tf_op jit(solution)/shard_map/all_gather | solution.py:374
  71.7 1.6 copy-start
  71.7 1.6 copy-start.8
  72.6 1.8 copy-start.9
  74.3 1.3 copy-start.1
  75.6 8.0 %copy-start.10 = (f32[16,4,8,128]{3,0,2,1:T(8,128)S(1)}, f32[16,4,8,128]{3,0,2,1:T(8,128)}, u32[]{:S(2)}) copy-start(f32[16,4,8,128]{3,0,2,1:T(8,128)} %copy-done.9) | copy-start | bytes 786436
  75.6 76.0 %all-to-all-start.2 = ((bf16[32,256,128]{2,1,0:T(8,128)(2,1)}), bf16[32,256,128]{2,1,0:T(8,128)(2,1)S(1)}, u32[]{:S(2)}, u32[]{:S(2)}) async-start(bf16[32,256,128]{2,1,0:T(8,128)(2,1)} %bitcast.61), calls=%async_computation.2 | async-start | bytes 4194304 | tf_op jit(solution)/shard_map/all_to_all | solution.py:409
  83.4 98.6 %all-gather.3.cloned.1.call-start = ((), (), s32[]{:S(2)}) async-start(), calls=%async_computation.5 | async-start | bytes 3342336 | tf_op jit(solution)/shard_map/all_gather | solution.py:375
  113.9 1.2 copy-start.6
  132.6 10.8 %collective-permute-start = (bf16[6,8,512]{2,1,0:T(8,128)(2,1)S(1)}, bf16[6,8,512]{2,1,0:T(8,128)(2,1)S(1)}, u32[]{:S(2)}, u32[]{:S(2)}) collective-permute-start(bf16[6,8,512]{2,1,0:T(8,128)(2,1)S(1)} %get-tuple-element.26), channel_id=1, source_target_pairs={{0,0},{1,16},{2,32},{3,48},{4,64},{5,80},{6,96},{7,112},{8,8},{9,2... | collective-permute-start | bytes 147464 | tf_op jit(solution)/shard_map/ppermute | solution.py:399
  140.6 11.0 %collective-permute-start.1 = (bf16[6,8,512]{2,1,0:T(8,128)(2,1)S(1)}, bf16[6,8,512]{2,1,0:T(8,128)(2,1)S(1)}, u32[]{:S(2)}, u32[]{:S(2)}) collective-permute-start(bf16[6,8,512]{2,1,0:T(8,128)(2,1)S(1)} %get-tuple-element.27), channel_id=1, source_target_pairs={{0,8},{1,24},{2,40},{3,56},{4,72},{5,88},{6,104},{7,120},{8,0},{9,... | collective-permute-start | bytes 147464 | tf_op jit(solution)/shard_map/ppermute | solution.py:400
  152.6 19.9 %all-to-all-start.3 = ((bf16[8,96,512]{2,1,0:T(8,128)(2,1)}), bf16[8,96,512]{2,1,0:T(8,128)(2,1)}, u32[]{:S(2)}, u32[]{:S(2)}) async-start(bf16[8,96,512]{2,1,0:T(8,128)(2,1)} %broadcast_in_dim.111), calls=%async_computation.3 | async-start | bytes 1572864 | tf_op jit(solution)/shard_map/all_to_all | solution.py:404
  173.1 1.4 copy-start.2
  174.5 36.8 %all-to-all-start.4 = ((bf16[16,512,128]{2,1,0:T(8,128)(2,1)}), bf16[16,512,128]{2,1,0:T(8,128)(2,1)S(1)}, u32[]{:S(2)}, u32[]{:S(2)}) async-start(bf16[16,512,128]{2,1,0:T(8,128)(2,1)} %bitcast.62), calls=%async_computation.4 | async-start | bytes 4194304 | tf_op jit(solution)/shard_map/all_to_all | solution.py:422
  182.0 1.9 copy-start.3
  193.1 1.2 copy-start.4
  194.2 1.1 copy-start.5
Sparse Core Ops, SparseCore 0:
  73.4 40.4 all-gather.4
  116.3 47.0 all-gather.2

commit v5 on v4

--- a/solution.py
+++ b/solution.py
@@ -371,6 +371,7 @@
         [front_piece.transpose(1, 0, 2, 3), diag_front.reshape(4, 4, PIECE, TILE)], axis=0
     )
     chunk = added + front_part.astype(F32)
+    chunk, first_tiles = lax.optimization_barrier((chunk, first_tiles))
     diag_all = lax.all_gather(chunk[12:].reshape(128, TILE), COL, axis=0)
     panel_all = lax.all_gather(chunk[:12].reshape(384, TILE), COL, axis=0)
     inverse = inverse_factor(diag_all)
@@ -401,12 +402,12 @@
     first = jnp.where(h_own == 0, same, cross)
     second = jnp.where(h_own == 0, cross, same)
     piece = jnp.concatenate([first, second], axis=1).reshape(96, KDIM)
+    message = first_tiles.reshape(32, 2 * TILE, TILE)
+    got = lax.all_to_all(message, ("xlo",) + COL, split_axis=0, concat_axis=0, tiled=True)
+    got, piece = lax.optimization_barrier((got, piece))
     trail = lax.all_to_all(
         jnp.broadcast_to(piece, (8, 96, KDIM)), ROW, split_axis=0, concat_axis=0, tiled=True
     )
-
-    message = first_tiles.reshape(32, 2 * TILE, TILE)
-    got = lax.all_to_all(message, ("xlo",) + COL, split_axis=0, concat_axis=0, tiled=True)
     got, trail = lax.optimization_barrier((got, trail))
     class_of = jnp.argmax(
         (maps[:, None, :8] % 8) == jnp.arange(8)[None, :, None], axis=2

time: 226 us -> 229 us (1.013)
  waiting for transfers between devices: 78.7 us -> 81.6 us
    all_gather x1, waiting for transfers between devices: 27.3 us -> 31.9 us  [per_device(): diag_all = lax.all_gather(chunk[12:].reshape(128, TILE), COL, axis=0)]
    ppermute x1, starting transfers between devices: 7.91 us -> 10.7 us  [per_device(): same = lax.ppermute(same, ROW + COL, route_same)]
    unnamed x23 -> x17, local copies, waits for them, and re-layouts: 8.11 us -> 6.79 us
where the time goes in v5:
time: 229 us; the launch traced here: 228 us
  waiting for transfers between devices  81.6 us (36%)
  Pallas kernels  45.7 us (20%)
  starting transfers between devices  34.8 us (15%)
  blocking collectives  31.7 us (14%)
  between operations  14.5 us (6%)
  local copies, waits for them, and re-layouts  13.4 us (6%)
  other arithmetic  4.79 us (2%)
    all_gather x1, waiting for transfers between devices, per_device(): diag_all = lax.all_gather(chunk[12:].reshape(128, TILE), COL, axis=0)  31.9 us
    all_to_all x1, blocking collectives, per_device(): got = lax.all_to_all(message, COL, split_axis=0, concat_axis=0, tiled=True)  31.7 us
    all_to_all x2, waiting for transfers between devices, per_device(): lax.all_to_all(message, ('front',) + ROW, split_axis=0, concat_axis=0, ti...  26 us
    pallas_call x1, Pallas kernels, inverse_factor(): pl.pallas_call(body, grid=(1,), out_shape=jax.ShapeDtypeStruct((KDIM, KDI...  16.3 us
    all_to_all x1, waiting for transfers between devices, per_device(): lax.all_to_all(jnp.broadcast_to(piece, (8, 96, KDIM)), ROW, split_axis=0,...  13.9 us
    all_to_all x2, starting transfers between devices, per_device(): lax.all_to_all(message, ('front',) + ROW, split_axis=0, concat_axis=0, ti...  10.8 us
    ppermute x1, starting transfers between devices, per_device(): same = lax.ppermute(same, ROW + COL, route_same)  10.7 us
    pallas_call x1, Pallas kernels, solve_rows(): pl.pallas_call(body, grid_spec=pltpu.PrefetchScalarGridSpec(num_scalar_pr...  9.18 us
  transfers between devices with their start and end apart: 8, of which 6 were waited for; matrix products, arithmetic and copies ran while one was open for 4% of the time, Pallas kernels for 16%

profile of v5, /device:TPU:32, one launch (start us, length us, event | category | flops | bytes accessed | tf_op | source)
XLA Modules:
  0.0 228.3 jit_solution(16331798432037460030)
XLA Ops:
  7.2 0.7 pad_add_fusion.2.place_ref
  7.9 3.2 %pack_panel.1 = bf16[16,224,128]{2,1,0:T(8,128)(2,1)} custom-call(s32[2]{0:T(128)} %pad_add_fusion.2.place_ref, s32[4,64]{1,0:T(4,128)} %bitcast.63, bf16[512,2048]{1,0:T(8,128)(2,1)} %child_ref.1, bf16[512,2048]{1,0:T(8,128)(2,1)} %child_ref.1, bf16[512,2048]{1,0:T(8,128)(2,1)} %child_ref.1, bf16[512,2048]{1,0:T(8,128)(2,1)} %child_ref.1, ...), custom_call_target="tpu_custom_call" | custom-call | tf_op jit(solution)/shard_map/pack_panel/pallas_call | solution.py:52
  11.0 31.7 %all_to_all.25 = bf16[16,224,128]{2,1,0:T(8,128)(2,1)S(1)} all-to-all(bf16[16,224,128]{2,1,0:T(8,128)(2,1)} %pack_panel.1), channel_id=1, replica_groups=mesh['front'=2,'rowh'=4,'xlo'=2,'z'=8,'core'=2] {'z','core'}, dimensions={0} | all-to-all | bytes 1835008 | tf_op jit(solution)/shard_map/all_to_all | solution.py:355
  42.7 0.1 bitcast_reduce_fusion
  42.9 1.2 broadcast_in_dim.108
  44.0 7.0 %all-to-all-start.1 = ((bf16[16,288,128]{2,1,0:T(8,128)(2,1)}), bf16[16,288,128]{2,1,0:T(8,128)(2,1)S(1)}, u32[]{:S(2)}, u32[]{:S(2)}) async-start(bf16[16,288,128]{2,1,0:T(8,128)(2,1)} %bitcast.13), calls=%async_computation.1 | async-start | bytes 2359296 | tf_op jit(solution)/shard_map/all_to_all | solution.py:363
  51.1 0.0 all-gather.5.cloned.1.call-start
  51.2 2.3 %pack_first.1 = bf16[64,128,128]{2,1,0:T(8,128)(2,1)} custom-call(s32[2]{0:T(128)S(1)} %copy-done.7, s32[4,64]{1,0:T(4,128)S(1)} %bitcast.64, bf16[512,2048]{1,0:T(8,128)(2,1)S(1)} %copy-done), custom_call_target="tpu_custom_call" | custom-call | bytes 4194304 | tf_op jit(solution)/shard_map/pack_first/pallas_call | solution.py:78
  53.5 0.1 eq.116
  53.5 0.1 copy.57
  53.6 0.1 pad_add_fusion.1
  53.8 18.0 %all-to-all-done.1 = bf16[16,288,128]{2,1,0:T(8,128)(2,1)S(1)} async-done(((bf16[16,288,128]{2,1,0:T(8,128)(2,1)}), bf16[16,288,128]{2,1,0:T(8,128)(2,1)S(1)}, u32[]{:S(2)}, u32[]{:S(2)}) %all-to-all-start.1) | async-done | bytes 1179680 | tf_op jit(solution)/shard_map/all_to_all | solution.py:363
  71.7 0.1 slice.56
  71.8 0.7 fusion
  72.6 0.6 copy.62
  73.3 7.6 %all-to-all-start.2 = ((bf16[32,256,128]{2,1,0:T(8,128)(2,1)}), bf16[32,256,128]{2,1,0:T(8,128)(2,1)S(1)}, u32[]{:S(2)}, u32[]{:S(2)}) async-start(bf16[32,256,128]{2,1,0:T(8,128)(2,1)} %bitcast.21), calls=%async_computation.2 | async-start | bytes 4194304 | tf_op jit(solution)/shard_map/all_to_all | solution.py:406
  80.9 0.2 all-gather.3.cloned.1.call-start
  81.2 0.7 copy.61
  82.0 0.1 broadcast_in_dim.112
  82.1 0.1 copy.66
  82.2 0.1 reshape.456
  82.3 0.7 iota_reduce_fusion
  83.0 0.8 gather_fusion
  83.8 0.1 gather.14
  83.9 0.1 broadcast_in_dim.109
  83.9 0.1 ge.21
  84.1 31.9 %all-gather.5.cloned.1.call-done.piece_ref = f32[16,128,128]{2,1,0:T(8,128)} async-done(((f32[1,128,128]{2,1,0:T(8,128)}), f32[16,128,128]{2,1,0:T(8,128)}) %all-gather.5.cloned.1.call-update) | async-done | bytes 1048592 | tf_op jit(solution)/shard_map/all_gather | solution.py:375
  116.0 1.2 copy-done.5
  117.2 16.3 %inverse_factor.1.w_ref = f32[512,512]{1,0:T(8,128)S(1)} custom-call(f32[16,128,128]{2,1,0:T(8,128)S(1)} %copy-done.5), custom_call_target="tpu_custom_call" | custom-call | tf_op jit(solution)/shard_map/inverse_factor/pallas_call | solution.py:190
  133.5 1.1 fusion.1
  134.7 10.7 %collective-permute-start = (bf16[6,8,512]{2,1,0:T(8,128)(2,1)S(1)}, bf16[6,8,512]{2,1,0:T(8,128)(2,1)S(1)}, u32[]{:S(2)}, u32[]{:S(2)}) collective-permute-start(bf16[6,8,512]{2,1,0:T(8,128)(2,1)S(1)} %get-tuple-element.34), channel_id=1, source_target_pairs={{0,0},{1,16},{2,32},{3,48},{4,64},{5,80},{6,96},{7,112},{8,8},{9,2... | collective-permute-start | bytes 147464 | tf_op jit(solution)/shard_map/ppermute | solution.py:400
  145.4 0.1 collective-permute-start.1
  145.5 3.0 %collective-permute-done = bf16[6,8,512]{2,1,0:T(8,128)(2,1)S(1)} collective-permute-done((bf16[6,8,512]{2,1,0:T(8,128)(2,1)S(1)}, bf16[6,8,512]{2,1,0:T(8,128)(2,1)S(1)}, u32[]{:S(2)}, u32[]{:S(2)}) %collective-permute-start) | collective-permute-done | bytes 49184 | tf_op jit(solution)/shard_map/ppermute | solution.py:400
  148.5 6.8 %collective-permute-done.1 = bf16[6,8,512]{2,1,0:T(8,128)(2,1)S(1)} collective-permute-done((bf16[6,8,512]{2,1,0:T(8,128)(2,1)S(1)}, bf16[6,8,512]{2,1,0:T(8,128)(2,1)S(1)}, u32[]{:S(2)}, u32[]{:S(2)}) %collective-permute-start.1) | collective-permute-done | bytes 49184 | tf_op jit(solution)/shard_map/ppermute | solution.py:401
  155.3 0.9 broadcast_in_dim.111
  156.3 5.4 %all-to-all-start.3 = ((bf16[8,96,512]{2,1,0:T(8,128)(2,1)}), bf16[8,96,512]{2,1,0:T(8,128)(2,1)}, u32[]{:S(2)}, u32[]{:S(2)}) async-start(bf16[8,96,512]{2,1,0:T(8,128)(2,1)} %broadcast_in_dim.111), calls=%async_computation.3 | async-start | bytes 1572864 | tf_op jit(solution)/shard_map/all_to_all | solution.py:408
  161.7 0.1 multiply_add_fusion
  161.8 0.1 add.301.index_ref
  161.9 0.6 compare_reduce_fusion.2
  162.5 13.9 %all-to-all-done.3.trail_ref = bf16[8,96,512]{2,1,0:T(8,128)(2,1)} async-done(((bf16[8,96,512]{2,1,0:T(8,128)(2,1)}), bf16[8,96,512]{2,1,0:T(8,128)(2,1)}, u32[]{:S(2)}, u32[]{:S(2)}) %all-to-all-start.3) | async-done | bytes 786464 | tf_op jit(solution)/shard_map/all_to_all | solution.py:408
  176.4 0.7 pack_second.1
  177.1 1.4 copy-done.1
  178.5 3.7 %all-to-all-start.4 = ((bf16[16,512,128]{2,1,0:T(8,128)(2,1)}), bf16[16,512,128]{2,1,0:T(8,128)(2,1)S(1)}, u32[]{:S(2)}, u32[]{:S(2)}) async-start(bf16[16,512,128]{2,1,0:T(8,128)(2,1)} %bitcast.61), calls=%async_computation.4 | async-start | bytes 4194304 | tf_op jit(solution)/shard_map/all_to_all | solution.py:423
  182.2 0.1 reshape.434
  182.3 0.1 copy.55
  182.4 0.1 copy.56
  182.5 0.2 or_reduce_fusion
  182.7 0.6 gather_fusion.1
  183.2 0.1 and_select_fusion
  183.3 0.2 slice_reduce_fusion
  183.5 1.4 compare_reduce_fusion
  185.0 0.1 iota_xor_fusion
  185.1 0.1 compare_select_fusion.3
  185.2 0.1 reshape.453.col_ref
  185.3 0.4 compare_reduce_fusion.1
  185.7 0.1 add_select_fusion
  185.8 0.1 select_n.198.at_ref
  186.0 1.9 copy-done.2
  187.9 9.2 %solve_rows.1 = (f32[1536,512]{1,0:T(8,128)}, bf16[1536,512]{1,0:T(8,128)(2,1)S(1)}, bf16[1536,512]{1,0:T(8,128)(2,1)S(1)}) custom-call(s32[1]{0:T(128)} %bitcast.4.tile_ref, f32[16,384,128]{2,1,0:T(8,128)S(1)} %copy-done.2, f32[512,512]{1,0:T(8,128)S(1)} %inverse_factor.1.w_ref), custom_call_target="tpu_custom_call" | custom-call | tf_op jit(solution)/shard_map/solve_rows/pallas_call | solution.py:238
  197.0 1.2 copy-done.3
  198.2 1.1 copy-done.4
  199.3 7.9 %trailing_update.1.base_ref = f32[1536,768]{1,0:T(8,128)} custom-call(bf16[1536,768]{1,0:T(8,128)(2,1)} %bitcast.69, bf16[1536,512]{1,0:T(8,128)(2,1)} %copy-done.3, bf16[1536,512]{1,0:T(8,128)(2,1)} %copy-done.4, bf16[8,96,512]{2,1,0:T(8,128)(2,1)} %all-to-all-done.3.trail_ref), custom_call_target="tpu_custom_call" | custom-call | tf_op jit(solution)/shard_map/trailing_update/pallas_call | solution.py:289
  207.2 8.0 %all-to-all-done.4 = bf16[16,512,128]{2,1,0:T(8,128)(2,1)S(1)} async-done(((bf16[16,512,128]{2,1,0:T(8,128)(2,1)}), bf16[16,512,128]{2,1,0:T(8,128)(2,1)S(1)}, u32[]{:S(2)}, u32[]{:S(2)}) %all-to-all-start.4) | async-done | bytes 2097184 | tf_op jit(solution)/shard_map/all_to_all | solution.py:423
  215.3 6.2 %add_tiles.1 = f32[1536,768]{1,0:T(8,128)} custom-call(s32[96]{0:T(128)S(1)} %select_n.198.at_ref, s32[96]{0:T(128)S(1)} %reshape.453.col_ref, f32[1536,768]{1,0:T(8,128)} %trailing_update.1.base_ref, bf16[64,128,128]{2,1,0:T(8,128)(2,1)S(1)} %bitcast.62), custom_call_target="tpu_custom_call", output_to_operand_aliasing={{}: (2, {})} | custom-call | tf_op jit(solution)/shard_map/add_tiles/pallas_call | solution.py:324
  (45 shorter events, 0.4 us)
Async XLA Ops:
  42.8 8.3 %copy-start = (bf16[512,2048]{1,0:T(8,128)(2,1)S(1)}, bf16[512,2048]{1,0:T(8,128)(2,1)}, u32[]{:S(2)}) copy-start(bf16[512,2048]{1,0:T(8,128)(2,1)} %child_ref.1) | copy-start | bytes 6291460
  42.8 8.3 %copy-start.6 = (s32[2,2,64]{2,1,0:T(2,128)S(1)}, s32[2,2,64]{2,1,0:T(2,128)}, u32[]{:S(2)}) copy-start(s32[2,2,64]{2,1,0:T(2,128)} %param.5) | copy-start | bytes 3076
  42.8 8.3 %copy-start.7 = (s32[2]{0:T(128)S(1)}, s32[2]{0:T(128)}, u32[]{:S(2)}) copy-start(s32[2]{0:T(128)} %pad_add_fusion.2.place_ref) | copy-start | bytes 28
  44.0 27.7 %all-to-all-start.1 = ((bf16[16,288,128]{2,1,0:T(8,128)(2,1)}), bf16[16,288,128]{2,1,0:T(8,128)(2,1)S(1)}, u32[]{:S(2)}, u32[]{:S(2)}) async-start(bf16[16,288,128]{2,1,0:T(8,128)(2,1)} %bitcast.13), calls=%async_computation.1 | async-start | bytes 2359296 | tf_op jit(solution)/shard_map/all_to_all | solution.py:363
  51.1 64.9 %all-gather.5.cloned.1.call-start = ((), (), s32[]{:S(2)}) async-start(), calls=%async_computation.6 | async-start | bytes 1114112 | tf_op jit(solution)/shard_map/all_gather | solution.py:375
  73.3 82.0 %all-to-all-start.2 = ((bf16[32,256,128]{2,1,0:T(8,128)(2,1)}), bf16[32,256,128]{2,1,0:T(8,128)(2,1)S(1)}, u32[]{:S(2)}, u32[]{:S(2)}) async-start(bf16[32,256,128]{2,1,0:T(8,128)(2,1)} %bitcast.21), calls=%async_computation.2 | async-start | bytes 4194304 | tf_op jit(solution)/shard_map/all_to_all | solution.py:406
  80.9 105.0 %all-gather.3.cloned.1.call-start = ((), (), s32[]{:S(2)}) async-start(), calls=%async_computation.5 | async-start | bytes 3342336 | tf_op jit(solution)/shard_map/all_gather | solution.py:376
  116.0 1.2 copy-start.5
  134.7 13.8 %collective-permute-start = (bf16[6,8,512]{2,1,0:T(8,128)(2,1)S(1)}, bf16[6,8,512]{2,1,0:T(8,128)(2,1)S(1)}, u32[]{:S(2)}, u32[]{:S(2)}) collective-permute-start(bf16[6,8,512]{2,1,0:T(8,128)(2,1)S(1)} %get-tuple-element.34), channel_id=1, source_target_pairs={{0,0},{1,16},{2,32},{3,48},{4,64},{5,80},{6,96},{7,112},{8,8},{9,2... | collective-permute-start | bytes 147464 | tf_op jit(solution)/shard_map/ppermute | solution.py:400
  145.4 9.9 %collective-permute-start.1 = (bf16[6,8,512]{2,1,0:T(8,128)(2,1)S(1)}, bf16[6,8,512]{2,1,0:T(8,128)(2,1)S(1)}, u32[]{:S(2)}, u32[]{:S(2)}) collective-permute-start(bf16[6,8,512]{2,1,0:T(8,128)(2,1)S(1)} %get-tuple-element.35), channel_id=1, source_target_pairs={{0,8},{1,24},{2,40},{3,56},{4,72},{5,88},{6,104},{7,120},{8,0},{9,... | collective-permute-start | bytes 147464 | tf_op jit(solution)/shard_map/ppermute | solution.py:401
  156.3 20.1 %all-to-all-start.3 = ((bf16[8,96,512]{2,1,0:T(8,128)(2,1)}), bf16[8,96,512]{2,1,0:T(8,128)(2,1)}, u32[]{:S(2)}, u32[]{:S(2)}) async-start(bf16[8,96,512]{2,1,0:T(8,128)(2,1)} %broadcast_in_dim.111), calls=%async_computation.3 | async-start | bytes 1572864 | tf_op jit(solution)/shard_map/all_to_all | solution.py:408
  177.1 1.4 copy-start.1
  178.5 36.8 %all-to-all-start.4 = ((bf16[16,512,128]{2,1,0:T(8,128)(2,1)}), bf16[16,512,128]{2,1,0:T(8,128)(2,1)S(1)}, u32[]{:S(2)}, u32[]{:S(2)}) async-start(bf16[16,512,128]{2,1,0:T(8,128)(2,1)} %bitcast.61), calls=%async_computation.4 | async-start | bytes 4194304 | tf_op jit(solution)/shard_map/all_to_all | solution.py:423
  186.0 1.9 copy-start.2
  197.0 1.2 copy-start.3
  198.2 1.1 copy-start.4
Sparse Core Ops, SparseCore 0:
  73.4 42.5 all-gather.4
  118.4 42.2 all-gather.2
